TPU v7x, 32 devices: a whole 2x2x4 slice. The times are simulated.
32 devices in a mesh: depth: 8 (over y, x, core), seq: 4 (over z).
Axes of the slice: x: 2, y: 2, z: 4, core: 2. Of those that a mesh axis runs over, the one named last changes fastest.
Arguments:
- interfaces: bfloat16 [8, 1, 2048, 1024], P('depth', None, 'seq'), may hold values from -6 to 6
- doc_ids: int32 [1, 2048], replicated, may hold values from 0 to 3, never falling along the last dimension, each value on 1 to 1024 neighbouring positions
- w_attn: bfloat16 [8, 1, 4, 1024, 1024], P('depth'), may hold values from -0.1875 to 0.1875
- w_up: bfloat16 [8, 1, 1024, 4096], P('depth'), may hold values from -0.1875 to 0.1875
- w_down: bfloat16 [8, 1, 4096, 1024], P('depth'), may hold values from -0.09375 to 0.09375
- norm_gains: float32 [8, 1, 2, 1024], P('depth'), may hold values from 0.25 to 1.75
- coarse_gain: float32 [8, 1024], P('depth'), may hold values from 0 to 1
Outputs:
- relaxed: bfloat16 [8, 1, 2048, 1024], P('depth', None, 'seq')
Inputs may be any that keep to these rules, and one draw needn't show every extreme that they name: doc_ids never fall along a sequence and number the documents packed into it.
All inputs are finite; a program needn't handle non-finite values.
Results may differ from a plain program's by a relative error of at most 0.025.
Values may be sent and summed in bfloat16 or wider, within the bound.
No kernel may reach another device: no remote copies, remote signals or barrier semaphores. Data moves between devices by JAX's collectives and lax.ppermute only.
A program may use at most 192 MiB of HBM per device.

v0:
```python
import functools

import jax
import jax.numpy as jnp
from jax import lax
from jax.experimental import pallas as pl
from jax.experimental.pallas import tpu as pltpu
from jax.sharding import PartitionSpec as P

HEADS = 16
LANES = 128
BLOCK = 256
TILE = 512
TILES = 2
VMEM_BYTES = 12 * 1024 * 1024
COST = pl.CostEstimate(flops=1 << 20, bytes_accessed=1 << 16, transcendentals=0)
F32 = jnp.float32
BF16 = jnp.bfloat16


def rms_norm(value, gain):
    return value * lax.rsqrt(jnp.mean(value * value, axis=-1, keepdims=True) + 1e-05) * gain


def dot(a, b):
    return jnp.dot(a, b, preferred_element_type=F32)


def attend(q_ref, k_ref, v_ref, num_ref, den_ref, column_ref, row_ref, doc_ref, q_at, k_at, causal=False):
    rows, width = q_ref.shape
    keys = k_ref.shape[0]
    head_dim = width // HEADS
    per_tile = LANES // head_dim
    q_block, k_block = min(BLOCK, rows), min(BLOCK, keys)
    lane = lax.broadcasted_iota(jnp.int32, (1, LANES), 1)
    members = [lane // head_dim == i for i in range(per_tile)]
    count_q, count_k = rows // q_block, keys // k_block

    def one(index, carry):
        qi, ki = index // count_k, index % count_k
        q0 = pl.multiple_of(qi * q_block, q_block)
        k0 = pl.multiple_of(ki * k_block, k_block)
        needed = doc_ref[0, k_at + k0 + k_block - 1] >= doc_ref[0, q_at + q0]
        if causal:
            needed = (k0 <= q0) & (needed | (k0 == q0))

        @pl.when(needed)
        def _():
            key_docs = row_ref[:, pl.ds(pl.multiple_of(k_at + k0, k_block), k_block)]
            allowed = column_ref[pl.ds(q0, q_block), :1] == key_docs
            if causal:
                q_pos = q0 + lax.broadcasted_iota(jnp.int32, (q_block, k_block), 0)
                k_pos = k0 + lax.broadcasted_iota(jnp.int32, (q_block, k_block), 1)
                allowed = allowed & (k_pos <= q_pos)
            ones = jnp.ones((k_block, LANES), BF16)

            def heads(tile, den):
                cols = pl.ds(pl.multiple_of(tile * LANES, LANES), LANES)
                queries = q_ref[pl.ds(q0, q_block), cols]
                keys_here = k_ref[pl.ds(k0, k_block), cols]
                values = jnp.concatenate([v_ref[pl.ds(k0, k_block), cols], ones], axis=1)
                num = None
                for i, member in enumerate(members):
                    scores = lax.dot_general(
                        jnp.where(member, queries, jnp.zeros_like(queries)),
                        keys_here,
                        (((1,), (1,)), ((), ())),
                        preferred_element_type=F32,
                    )
                    weights = jnp.where(allowed, jnp.exp(scores), 0.0).astype(BF16)
                    out = dot(weights, values)
                    num = out[:, :LANES] if num is None else jnp.where(member, out[:, :LANES], num)
                    den = jnp.where(lane == tile * per_tile + i, out[:, LANES:], den)
                num_ref[pl.ds(q0, q_block), cols] += num
                return den

            def some(step, den):
                for i in range(TILES):
                    den = heads(step * TILES + i, den)
                return den

            den = jnp.zeros((q_block, LANES), F32)
            den_ref[pl.ds(q0, q_block), :] += lax.fori_loop(0, width // LANES // TILES, some, den)

        return carry

    lax.fori_loop(0, count_q * count_k, one, 0)


def spread(per_head, width):
    shape = (LANES, width)
    chosen = lax.broadcasted_iota(jnp.int32, shape, 1) // (width // HEADS) == lax.broadcasted_iota(jnp.int32, shape, 0)
    chosen = jnp.where(chosen, 1.0, 0.0).astype(BF16)
    high = per_head.astype(BF16)
    return dot(high, chosen) + dot((per_head - high.astype(F32)).astype(BF16), chosen)


def normed(x_ref, gain_ref):
    return rms_norm(x_ref[...].astype(F32), gain_ref[0:1]).astype(BF16)


def project(n_ref, w_ref, index, out_ref, scale=None):
    width = w_ref.shape[2]
    tile = min(TILE, width)

    def one(j, carry):
        cols = pl.ds(pl.multiple_of(j * tile, tile), tile)
        out = dot(n_ref[...], w_ref[index, :, cols]).astype(BF16)
        out_ref[:, cols] = out if scale is None else out * jnp.asarray(scale, BF16)
        return carry

    lax.fori_loop(0, width // tile, one, 0)


def own_kernel(
    x_ref, gain_ref, w_ref, column_ref, row_ref, doc_ref, q_ref, num_ref, den_ref, n_ref, k_ref, v_ref
):
    head_dim = x_ref.shape[1] // HEADS
    here = lax.axis_index("seq") * x_ref.shape[0]
    n_ref[...] = normed(x_ref, gain_ref)
    project(n_ref, w_ref, 0, q_ref, head_dim ** (-0.5))
    project(n_ref, w_ref, 1, k_ref)
    project(n_ref, w_ref, 2, v_ref)
    num_ref[...] = jnp.zeros_like(num_ref)
    den_ref[...] = jnp.zeros_like(den_ref)
    attend(q_ref, k_ref, v_ref, num_ref, den_ref, column_ref, row_ref, doc_ref, here, here, True)


def piece_kernel(
    shift, first, x_ref, gain_ref, w_ref, q_ref, num_in, den_in, column_ref, row_ref, doc_ref,
    num_ref, den_ref, n_ref, k_ref, v_ref,
):
    del num_in, den_in
    rows, keys = q_ref.shape[0], x_ref.shape[0]
    shard = lax.axis_index("seq") - shift
    here, there = (shard + shift) * rows, jnp.maximum(shard, 0) * rows + first

    @pl.when((shard >= 0) & (doc_ref[0, there + keys - 1] >= doc_ref[0, here]))
    def _():
        n_ref[...] = normed(x_ref, gain_ref)
        project(n_ref, w_ref, 1, k_ref)
        project(n_ref, w_ref, 2, v_ref)
        attend(q_ref, k_ref, v_ref, num_ref, den_ref, column_ref, row_ref, doc_ref, here, there)


def far_document(doc_ref, rows, count):
    found = False
    for middle in range(1, count - 1):
        over = doc_ref[0, middle * rows - 1] == doc_ref[0, (middle + 1) * rows]
        deep = doc_ref[0, middle * rows - rows // 2 - 1] == doc_ref[0, (middle + 1) * rows]
        found = found | (over & deep)
    return found


def message_kernel(
    x_ref, piece_ref, gain_ref, w_ref, column_ref, row_ref, doc_ref,
    out_ref, q_ref, n_ref, k_ref, v_ref, num_ref, den_ref,
):
    half, width = x_ref.shape
    rows = 2 * half
    count = lax.axis_size("seq")
    place = lax.axis_index("seq")
    inside = (place >= 1) & (place + 1 < count)
    here = jnp.where(inside, place + 1, 0) * rows
    there = jnp.where(inside, place - 1, 0) * rows
    far = far_document(doc_ref, rows, count)

    @pl.when(jnp.logical_not(far))
    def _():
        out_ref[:, :width] = piece_ref[half:]

    @pl.when(far)
    def _():
        num_ref[...] = jnp.zeros_like(num_ref)
        den_ref[...] = jnp.zeros_like(den_ref)

        @pl.when(inside & (doc_ref[0, there + rows - 1] >= doc_ref[0, here]))
        def _():
            n_ref[:half] = normed(x_ref, gain_ref)
            project(n_ref.at[:half], w_ref, 0, q_ref, (width // HEADS) ** (-0.5))
            n_ref[...] = normed(piece_ref, gain_ref)
            project(n_ref, w_ref, 1, k_ref)
            project(n_ref, w_ref, 2, v_ref)
            attend(q_ref, k_ref, v_ref, num_ref, den_ref, column_ref, row_ref, doc_ref, here, there)

        out_ref[:, :width] = num_ref[...].astype(BF16)
        out_ref[:, width:] = den_ref[...].astype(BF16)


def reply_kernel(
    message_ref, gain_ref, w_ref, q_ref, num_in, den_in, column_ref, row_ref, doc_ref,
    num_ref, den_ref, n_ref, k_ref, v_ref,
):
    rows, width = q_ref.shape
    half = message_ref.shape[0]
    far = far_document(doc_ref, rows, lax.axis_size("seq"))

    @pl.when(far)
    def _():
        num_ref[:half] += message_ref[:, :width].astype(F32)
        den_ref[:half] += message_ref[:, width:].astype(F32)

    @pl.when(jnp.logical_not(far))
    def _():
        piece_kernel(
            2, half, message_ref.at[:, :width], gain_ref, w_ref, q_ref, num_in, den_in, column_ref, row_ref, doc_ref,
            num_ref, den_ref, n_ref, k_ref, v_ref,
        )


def finish_kernel(
    first, x_ref, num_ref, den_ref, w_ref, gain_ref, up_ref, down_ref, out_ref, acc_ref, n_ref, hidden_ref
):
    rows, width = out_ref.shape
    hidden = up_ref.shape[1]
    tile = min(TILE, hidden)
    here = pl.ds(first, rows)
    lane = lax.broadcasted_iota(jnp.int32, (rows, LANES), 1)
    inverse = 1.0 / jnp.where(lane < HEADS, den_ref[here], 1.0)
    n_ref[...] = (num_ref[here] * spread(inverse, width)).astype(BF16)
    acc_ref[...] = x_ref[here].astype(F32) + dot(n_ref[...], w_ref[3])
    n_ref[...] = rms_norm(acc_ref[...], gain_ref[1:2]).astype(BF16)

    def expand(j):
        cols = pl.ds(pl.multiple_of(j * tile, tile), tile)
        return jax.nn.gelu(dot(n_ref[...], up_ref[:, cols])).astype(BF16)

    def lower(j, expanded):
        return dot(expanded, down_ref[pl.ds(pl.multiple_of(j * tile, tile), tile)])

    hidden_ref[0] = expand(0)

    def one(j, carry):
        expanded = expand(j + 1)
        acc_ref[...] += lower(j, hidden_ref[j % 2])
        hidden_ref[(j + 1) % 2] = expanded
        return carry

    last = hidden // tile - 1
    lax.fori_loop(0, last, one, 0)
    out_ref[...] = (acc_ref[...] + lower(last, hidden_ref[last % 2])).astype(BF16)


def vmem():
    return pl.BlockSpec(memory_space=pltpu.VMEM)


def call(kernel, name, operands, docs, results, scratch, aliases=None, held=True):
    inputs = [pltpu.with_memory_space_constraint(operand, pltpu.VMEM) for operand in operands]
    in_specs = [vmem()] * len(inputs)
    if docs is not None:
        inputs.append(docs)
        in_specs.append(pl.BlockSpec(memory_space=pltpu.SMEM))
    return pl.pallas_call(
        kernel,
        in_specs=in_specs,
        out_specs=[vmem()] * len(results),
        out_shape=[pltpu.VMEM(*one) if held else jax.ShapeDtypeStruct(*one) for one in results],
        scratch_shapes=scratch,
        input_output_aliases=aliases or {},
        compiler_params=pltpu.CompilerParams(vmem_limit_bytes=VMEM_BYTES),
        cost_estimate=COST,
        name=name,
    )(*inputs)


def own_part(x, gains, weights, docs):
    rows, width = x.shape
    results = [((rows, width), BF16), ((rows, width), F32), ((rows, LANES), F32)]
    scratch = [pltpu.VMEM((rows, width), BF16)] * 3
    return call(own_kernel, "own_part", (x, gains, weights[0], docs.own_column, docs.ids), docs.ids, results, scratch)


def piece_part(x, shift, gains, w_attn, q, num, den, docs):
    rows, width = q.shape
    return call(
        functools.partial(piece_kernel, shift, 0),
        "piece_part",
        (x, gains, w_attn, q, num, den, docs.own_column, docs.ids),
        docs.ids,
        [((rows, width), F32), ((rows, LANES), F32)],
        [pltpu.VMEM((x.shape[0], width), BF16)] * 3,
        aliases={4: 0, 5: 1},
    )


def message_part(x, piece, gains, w_attn, docs):
    half, width = x.shape
    keys = 2 * half
    return call(
        message_kernel,
        "message_part",
        (x, piece, gains, w_attn, docs.later_column, docs.ids),
        docs.ids,
        [((half, width + LANES), BF16)],
        [pltpu.VMEM((half, width), BF16)]
        + [pltpu.VMEM((keys, width), BF16)] * 3
        + [pltpu.VMEM((half, width), F32), pltpu.VMEM((half, LANES), F32)],
    )[0]


def reply_part(message, gains, w_attn, q, num, den, docs):
    rows, width = q.shape
    return call(
        reply_kernel,
        "reply_part",
        (message, gains, w_attn, q, num, den, docs.own_column, docs.ids),
        docs.ids,
        [((rows, width), F32), ((rows, LANES), F32)],
        [pltpu.VMEM((message.shape[0], width), BF16)] * 3,
        aliases={4: 0, 5: 1},
    )


def finish_part(x, num, den, weights, gains, part, parts):
    width = x.shape[1]
    rows = x.shape[0] // parts
    w_attn, w_up, w_down = weights
    tile = min(TILE, w_up.shape[1])
    return call(
        functools.partial(finish_kernel, part * rows),
        "finish_part",
        (x, num, den, w_attn, gains, w_up, w_down),
        None,
        [((rows, width), BF16)],
        [pltpu.VMEM((rows, width), F32), pltpu.VMEM((rows, width), BF16), pltpu.VMEM((2, rows, tile), BF16)],
        held=parts > 1,
    )[0]


def shifted(value, axis, steps):
    count = lax.axis_size(axis)
    first, last = max(0, -steps), min(count, count - steps)
    return lax.ppermute(value, axis, [(i, i + steps) for i in range(first, last)])


def swapped(value, axis, bit):
    return lax.ppermute(value, axis, [(i, i ^ bit) for i in range(lax.axis_size(axis))])


class Documents:
    def __init__(self, doc_ids, rows):
        count = lax.axis_size("seq")
        self.ids, self.rows, self.half = doc_ids, rows, rows // 2
        longest = doc_ids.shape[1] // 2
        self.hops = min(count - 1, -(-(longest - 1) // rows))
        self.short = self.hops == 2 and longest <= 2 * rows and rows % 2 == 0
        place = lax.axis_index("seq")

        def column(later, size):
            start = jnp.minimum((place + later) * rows, doc_ids.shape[1] - size)
            ids = lax.dynamic_slice_in_dim(doc_ids, start, size, 1)
            return jnp.broadcast_to(ids.reshape(-1, 1), (size, LANES))

        self.own_column = column(0, rows)
        self.later_column = column(1, self.half) if self.short else self.own_column


def attention(state, piece, first_back, docs, gains, w_attn):
    q, *state = state
    if docs.short:
        message = shifted(message_part(after(first_back, q), piece, gains, w_attn, docs), "seq", 1)
        num, den = piece_part(piece, 1, gains, w_attn, q, *state, docs)
        return reply_part(message, gains, w_attn, q, num, den, docs)
    state = piece_part(piece, 1, gains, w_attn, q, *state, docs)
    for hop in range(2, docs.hops + 1):
        piece = shifted(piece, "seq", 1)
        state = piece_part(piece, hop, gains, w_attn, q, *state, docs)
    return state


def gain_factors(gain, bits):
    count = lax.axis_size("depth")
    all_gains = [gain] + [swapped(gain, "depth", i) for i in range(1, max(2, count // 2))]

    def block(first, size):
        return functools.reduce(jnp.multiply, all_gains[first : first + size])

    even_gain = jnp.where(bits[1], all_gains[1], gain)
    odd_gain = jnp.where(bits[1], gain, all_gains[1])
    factor_before, levels, bit = jnp.ones_like(gain), [], 2
    while bit < count:
        mine = block(0, bit)
        theirs = block(bit, bit) if 2 * bit < count else mine
        levels.append((bit, mine, theirs, factor_before))
        if 2 * bit < count:
            factor_before = jnp.where(bits[bit], factor_before * theirs, factor_before)
        bit *= 2
    return even_gain, odd_gain, levels


def after(value, *earlier):
    return lax.optimization_barrier((value, *earlier))[0]


class Chain:
    def __init__(self, states, following, factors, bits):
        self.states, self.following, self.bits = states, following, bits
        self.even_gain, self.odd_gain, self.levels = factors
        self.odd = bits[1]

    def enter(self, fine, *earlier):
        half = fine.shape[0] // 2
        mismatch = after(fine, *earlier).astype(F32) - self.following.astype(F32)
        low, high = mismatch[:half], mismatch[half:]
        mine = jnp.where(self.odd, high, low)
        sent = jnp.where(self.odd, low, high).astype(BF16)
        other = swapped(sent, "depth", 1).astype(F32)
        self.m_even = jnp.where(self.odd, other, mine)
        self.total = self.odd_gain * self.m_even + jnp.where(self.odd, mine, other)
        self.before = jnp.zeros_like(self.total)
        self.entered = self.total

    def level(self, index, sent_after=(), used_after=()):
        bit, factor, their_factor, factor_before = self.levels[index]
        upper = self.bits[bit]
        sent = after(self.total.astype(BF16), *sent_after)
        theirs = after(swapped(sent, "depth", bit), *used_after).astype(F32)
        if index + 1 < len(self.levels):
            self.total = jnp.where(upper, factor * theirs + self.total, their_factor * self.total + theirs)
        self.before = jnp.where(upper, factor_before * theirs + self.before, self.before)

    def leave(self, used_after=()):
        odd, c_even = self.odd, self.before
        c_odd = self.even_gain * c_even + self.m_even
        mine = jnp.where(odd, c_odd, c_even)
        other = swapped(jnp.where(odd, c_even, c_odd).astype(BF16), "depth", 1)
        other = after(other, *used_after).astype(F32)
        correction = jnp.concatenate([jnp.where(odd, other, mine), jnp.where(odd, mine, other)], axis=0)
        return (self.states.astype(F32) + correction).astype(BF16)


def on_device(interfaces, doc_ids, w_attn, w_up, w_down, norm_gains, coarse_gain):
    x = interfaces[0, 0]
    rows = x.shape[0]
    half = rows // 2
    gains = norm_gains[0, 0]
    weights = (w_attn[0, 0], w_up[0, 0], w_down[0, 0])
    parts = [x[:half], x[half:]]
    piece = shifted(x, "seq", 1)
    first_back = shifted(parts[0], "seq", -1)
    docs = Documents(doc_ids, rows)
    place, bits, bit = lax.axis_index("depth"), {}, 1
    while bit < lax.axis_size("depth"):
        bits[bit] = (place & bit) != 0
        bit *= 2
    early, bits, docs.own_column, docs.later_column = lax.optimization_barrier(
        (x, bits, docs.own_column, docs.later_column)
    )
    factors = gain_factors(after(coarse_gain, docs.own_column), bits)
    state = own_part(after(early, *jax.tree.leaves(factors)), gains, weights, docs)
    following = shifted(after(x, state[0]), "depth", -1)
    num, den = attention(state, piece, first_back, docs, gains, weights[0])
    following = [following[:half], following[half:]]
    first, second = [Chain(parts[i], following[i], factors, bits) for i in range(2)]
    first.enter(finish_part(x, num, den, weights, gains, 0, 2))
    fine = finish_part(x, after(num, first.total), den, weights, gains, 1, 2)
    first.level(0)
    second.enter(fine, first.total)
    for i in range(1, len(first.levels)):
        second.level(i - 1)
        first.level(i, used_after=(second.entered,))
    corrected = [first.leave()]
    halves = [shifted(corrected[0], "seq", 1)]
    first_back = shifted(corrected[0], "seq", -1)
    second.level(len(first.levels) - 1, sent_after=(corrected[0],))
    corrected.append(second.leave(used_after=(halves[0],)))
    halves.append(shifted(corrected[1], "seq", 1))
    x = jnp.concatenate(corrected, axis=0)
    state = own_part(x, gains, weights, docs)
    piece = jnp.concatenate(halves, axis=0)
    num, den = attention(state, piece, first_back, docs, gains, weights[0])
    return finish_part(x, num, den, weights, gains, 0, 1)[None, None]


def solution(mesh):
    in_specs = (
        P("depth", None, "seq", None),
        P(),
        P("depth", None, None, None, None),
        P("depth", None, None, None),
        P("depth", None, None, None),
        P("depth", None, None, None),
        P("depth", None),
    )
    out_specs = P("depth", None, "seq", None)
    return jax.shard_map(
        on_device, mesh=mesh, in_specs=in_specs, out_specs=out_specs, check_vma=False
    )
```

profile of v0, /device:TPU:8, one launch (start us, length us, event | category | flops | bytes accessed | tf_op | source)
XLA Modules:
  0.0 169.3 jit_solution(1606842931622267661)
XLA Ops:
  0.0 0.8 constant_dynamic-slice_fusion.1
  0.8 0.8 constant_dynamic-slice_fusion
  1.5 0.1 broadcast_in_dim.21.column_ref
  1.6 0.1 broadcast_in_dim.23.column_ref
  1.7 0.1 collective-permute-start.2
  1.8 1.6 collective-permute-start
  3.4 0.3 collective-permute-start.1
  3.7 3.5 %collective-permute-start.4 = (bf16[512,1024]{1,0:T(8,128)(2,1)}, bf16[512,1024]{1,0:T(8,128)(2,1)S(1)}, u32[]{:S(2)}, u32[]{:S(2)}) collective-permute-start(bf16[512,1024]{1,0:T(8,128)(2,1)} %bitcast.1.x_ref), channel_id=1, source_target_pairs={{0,1},{1,2},{2,3},{4,5},{5,6},{6,7},{8,9},{9,10},{10,11},{12,13},{... | collective-permute-start | bytes 3145736 | tf_op jit(solution)/shard_map/ppermute | solution.py:334
  7.2 1.1 slice_bitcast_fusion
  8.3 2.4 %collective-permute-start.3 = (bf16[256,1024]{1,0:T(8,128)(2,1)S(1)}, bf16[256,1024]{1,0:T(8,128)(2,1)S(1)}, u32[]{:S(2)}, u32[]{:S(2)}) collective-permute-start(bf16[256,1024]{1,0:T(8,128)(2,1)S(1)} %slice_bitcast_fusion), channel_id=1, source_target_pairs={{1,0},{2,1},{3,2},{5,4},{6,5},{7,6},{9,8},{10,9},{11,10},{13,12},{... | collective-permute-start | bytes 1572872 | tf_op jit(solution)/shard_map/ppermute | solution.py:334
  10.7 0.7 fusion.15
  11.4 3.4 %copy-done = bf16[1,1,4,1024,1024]{4,3,2,1,0:T(8,128)(2,1)S(1)} copy-done((bf16[1,1,4,1024,1024]{4,3,2,1,0:T(8,128)(2,1)S(1)}, bf16[1,1,4,1024,1024]{4,3,2,1,0:T(8,128)(2,1)}, u32[]{:S(2)}) %copy-start) | copy-done | bytes 8388632
  14.8 0.7 copy-done.2
  15.5 0.7 copy-done.4
  16.2 13.3 %own_part.2 = (bf16[512,1024]{1,0:T(8,128)(2,1)S(1)}, f32[512,1024]{1,0:T(8,128)S(1)}, f32[512,128]{1,0:T(8,128)S(1)}) custom-call(bf16[512,1024]{1,0:T(8,128)(2,1)} %bitcast.1.x_ref, f32[2,1024]{1,0:T(2,128)S(1)} %bitcast.41, bf16[4,1024,1024]{2,1,0:T(8,128)(2,1)S(1)} %bitcast.20, s32[512,128]{1,0:T(8,128)S(1)} %broadcast_in_dim.21.column_ref, ...), custom_call_target="tpu_custom_call" | custom-call | flops 1048576 | bytes 65536 | tf_op jit(solution)/shard_map/own_part/pallas_call | solution.py:254
  29.5 1.3 collective-permute-start.6
  30.8 0.4 collective-permute-done.4.piece_ref.x_ref
  31.2 0.8 message_part.2
  32.0 12.5 %collective-permute-start.5 = (bf16[256,1152]{1,0:T(8,128)(2,1)S(1)}, bf16[256,1152]{1,0:T(8,128)(2,1)S(1)}, u32[]{:S(2)}, u32[]{:S(2)}) collective-permute-start(bf16[256,1152]{1,0:T(8,128)(2,1)S(1)} %message_part.2), channel_id=1, source_target_pairs={{0,1},{1,2},{2,3},{4,5},{5,6},{6,7},{8,9},{9,10},{10,11},{12,13},{... | collective-permute-start | bytes 1769480 | tf_op jit(solution)/shard_map/ppermute | solution.py:334
  44.6 0.0 slice-start.1
  44.6 6.3 %piece_part.2 = (f32[512,1024]{1,0:T(8,128)S(1)}, f32[512,128]{1,0:T(8,128)S(1)}) custom-call(bf16[512,1024]{1,0:T(8,128)(2,1)S(1)} %collective-permute-done.4.piece_ref.x_ref, f32[2,1024]{1,0:T(2,128)S(1)} %bitcast.43, bf16[4,1024,1024]{2,1,0:T(8,128)(2,1)S(1)} %bitcast.22, ...), custom_call_target="tpu_custom_call", output_to_operand_aliasing={{0}: (4, {}), {1}: (5, {})} | custom-call | flops 1048576 | bytes 65536 | tf_op jit(solution)/shard_map/piece_part/pallas_call | solution.py:254
  50.9 7.1 %collective-permute-done.5.message_ref = bf16[256,1152]{1,0:T(8,128)(2,1)S(1)} collective-permute-done((bf16[256,1152]{1,0:T(8,128)(2,1)S(1)}, bf16[256,1152]{1,0:T(8,128)(2,1)S(1)}, u32[]{:S(2)}, u32[]{:S(2)}) %collective-permute-start.5) | collective-permute-done | bytes 589856 | tf_op jit(solution)/shard_map/ppermute | solution.py:334
  58.0 1.0 reply_part.2
  59.0 9.3 %finish_part.3 = bf16[256,1024]{1,0:T(8,128)(2,1)S(1)} custom-call(bf16[512,1024]{1,0:T(8,128)(2,1)} %bitcast.1.x_ref, f32[512,1024]{1,0:T(8,128)S(1)} %get-tuple-element.52.num_ref, f32[512,128]{1,0:T(8,128)S(1)} %get-tuple-element.50.den_ref, bf16[4,1024,1024]{2,1,0:T(8,128)(2,1)S(1)} %bitcast.24, f32[2,1024]{1,0:T(2,128)S(1)} %bitcast.45, ...), custom_call_target="tpu_custom_call" | custom-call | flops 1048576 | bytes 65536 | tf_op jit(solution)/shard_map/finish_part/pallas_call | solution.py:254
  68.3 0.2 convert_subtract_fusion.1
  68.5 0.1 select_convert_fusion.3
  68.5 0.1 collective-permute-start.7
  68.6 1.5 collective-permute-done.7
  70.1 0.2 fusion.13
  70.3 1.6 collective-permute-start.8
  71.9 9.4 %finish_part.4 = bf16[256,1024]{1,0:T(8,128)(2,1)S(1)} custom-call(bf16[512,1024]{1,0:T(8,128)(2,1)} %bitcast.1.x_ref, f32[512,1024]{1,0:T(8,128)S(1)} %get-tuple-element.52.num_ref, f32[512,128]{1,0:T(8,128)S(1)} %get-tuple-element.50.den_ref, bf16[4,1024,1024]{2,1,0:T(8,128)(2,1)S(1)} %bitcast.25, f32[2,1024]{1,0:T(2,128)S(1)} %bitcast.46, ...), custom_call_target="tpu_custom_call" | custom-call | flops 1048576 | bytes 65536 | tf_op jit(solution)/shard_map/finish_part/pallas_call | solution.py:254
  81.3 0.1 fusion.5
  81.4 0.2 convert_subtract_fusion
  81.6 0.1 select_convert_fusion.2
  81.6 0.1 collective-permute-start.10
  81.7 1.7 collective-permute-start.9
  83.4 0.2 fusion.11
  83.6 0.4 collective-permute-start.12
  84.0 6.4 %collective-permute-done.9 = bf16[128,1024]{1,0:T(8,128)(2,1)S(1)} collective-permute-done((bf16[128,1024]{1,0:T(8,128)(2,1)S(1)}, bf16[128,1024]{1,0:T(8,128)(2,1)S(1)}, u32[]{:S(2)}, u32[]{:S(2)}) %collective-permute-start.9) | collective-permute-done | bytes 262176 | tf_op jit(solution)/shard_map/ppermute | solution.py:338
  90.4 0.2 select_convert_fusion.1
  90.6 0.1 collective-permute-start.11
  90.7 1.3 collective-permute-done.12
  92.0 0.1 fusion.8
  92.1 0.1 collective-permute-done.11
  92.2 0.3 convert_select_fusion.5
  92.5 1.2 fusion
  93.7 1.7 collective-permute-start.13
  95.4 4.5 %collective-permute-start.15 = (bf16[256,1024]{1,0:T(8,128)(2,1)S(1)}, bf16[256,1024]{1,0:T(8,128)(2,1)S(1)}, u32[]{:S(2)}, u32[]{:S(2)}) collective-permute-start(bf16[256,1024]{1,0:T(8,128)(2,1)S(1)} %fusion), channel_id=1, source_target_pairs={{0,1},{1,2},{2,3},{4,5},{5,6},{6,7},{8,9},{9,10},{10,11},{12,13},{... | collective-permute-start | bytes 1572872 | tf_op jit(solution)/shard_map/ppermute | solution.py:334
  99.8 2.3 %collective-permute-done.13 = bf16[128,1024]{1,0:T(8,128)(2,1)S(1)} collective-permute-done((bf16[128,1024]{1,0:T(8,128)(2,1)S(1)}, bf16[128,1024]{1,0:T(8,128)(2,1)S(1)}, u32[]{:S(2)}, u32[]{:S(2)}) %collective-permute-start.13) | collective-permute-done | bytes 262176 | tf_op jit(solution)/shard_map/ppermute | solution.py:338
  102.1 0.2 select_convert_fusion
  102.3 0.1 collective-permute-start.14
  102.4 1.9 %collective-permute-start.16 = (bf16[256,1024]{1,0:T(8,128)(2,1)S(1)}, bf16[256,1024]{1,0:T(8,128)(2,1)S(1)}, u32[]{:S(2)}, u32[]{:S(2)}) collective-permute-start(bf16[256,1024]{1,0:T(8,128)(2,1)S(1)} %fusion), channel_id=1, source_target_pairs={{1,0},{2,1},{3,2},{5,4},{6,5},{7,6},{9,8},{10,9},{11,10},{13,12},{... | collective-permute-start | bytes 1572872 | tf_op jit(solution)/shard_map/ppermute | solution.py:334
  104.3 6.7 %collective-permute-done.15 = bf16[256,1024]{1,0:T(8,128)(2,1)S(1)} collective-permute-done((bf16[256,1024]{1,0:T(8,128)(2,1)S(1)}, bf16[256,1024]{1,0:T(8,128)(2,1)S(1)}, u32[]{:S(2)}, u32[]{:S(2)}) %collective-permute-start.15) | collective-permute-done | bytes 524320 | tf_op jit(solution)/shard_map/ppermute | solution.py:334
  111.0 0.3 convert_select_fusion.3
  111.3 1.2 fusion.1
  112.5 4.4 %collective-permute-start.17 = (bf16[256,1024]{1,0:T(8,128)(2,1)S(1)}, bf16[256,1024]{1,0:T(8,128)(2,1)S(1)}, u32[]{:S(2)}, u32[]{:S(2)}) collective-permute-start(bf16[256,1024]{1,0:T(8,128)(2,1)S(1)} %fusion.1), channel_id=1, source_target_pairs={{0,1},{1,2},{2,3},{4,5},{5,6},{6,7},{8,9},{9,10},{10,11},{12,13},{... | collective-permute-start | bytes 1572872 | tf_op jit(solution)/shard_map/ppermute | solution.py:334
  116.9 0.1 pad_maximum_fusion.x_ref
  117.0 12.6 %own_part.3 = (bf16[512,1024]{1,0:T(8,128)(2,1)S(1)}, f32[512,1024]{1,0:T(8,128)S(1)}, f32[512,128]{1,0:T(8,128)S(1)}) custom-call(bf16[512,1024]{1,0:T(8,128)(2,1)S(1)} %pad_maximum_fusion.x_ref, f32[2,1024]{1,0:T(2,128)S(1)} %bitcast.47, bf16[4,1024,1024]{2,1,0:T(8,128)(2,1)S(1)} %bitcast.26, s32[512,128]{1,0:T(8,128)S(1)} %broadcast_in_dim.21.column_ref, ...), custom_call_target="tpu_custom_call" | custom-call | flops 1048576 | bytes 65536 | tf_op jit(solution)/shard_map/own_part/pallas_call | solution.py:254
  129.7 1.0 message_part.3
  130.7 11.2 %collective-permute-start.18 = (bf16[256,1152]{1,0:T(8,128)(2,1)S(1)}, bf16[256,1152]{1,0:T(8,128)(2,1)S(1)}, u32[]{:S(2)}, u32[]{:S(2)}) collective-permute-start(bf16[256,1152]{1,0:T(8,128)(2,1)S(1)} %message_part.3), channel_id=1, source_target_pairs={{0,1},{1,2},{2,3},{4,5},{5,6},{6,7},{8,9},{9,10},{10,11},{12,13},{... | collective-permute-start | bytes 1769480 | tf_op jit(solution)/shard_map/ppermute | solution.py:334
  141.9 6.3 %piece_part.3 = (f32[512,1024]{1,0:T(8,128)S(1)}, f32[512,128]{1,0:T(8,128)S(1)}) custom-call(bf16[512,1024]{1,0:T(8,128)(2,1)S(1)} %constant_dynamic-update-slice_fusion.piece_ref.x_ref, f32[2,1024]{1,0:T(2,128)S(1)} %bitcast.49, bf16[4,1024,1024]{2,1,0:T(8,128)(2,1)S(1)} %bitcast.28, ...), custom_call_target="tpu_custom_call", output_to_operand_aliasing={{0}: (4, {}), {1}: (5, {})} | custom-call | flops 1048576 | bytes 65536 | tf_op jit(solution)/shard_map/piece_part/pallas_call | solution.py:254
  148.3 5.2 %collective-permute-done.18.message_ref = bf16[256,1152]{1,0:T(8,128)(2,1)S(1)} collective-permute-done((bf16[256,1152]{1,0:T(8,128)(2,1)S(1)}, bf16[256,1152]{1,0:T(8,128)(2,1)S(1)}, u32[]{:S(2)}, u32[]{:S(2)}) %collective-permute-start.18) | collective-permute-done | bytes 589856 | tf_op jit(solution)/shard_map/ppermute | solution.py:334
  153.5 0.8 reply_part.3
  154.3 15.1 %finish_part.5 = bf16[512,1024]{1,0:T(8,128)(2,1)} custom-call(bf16[512,1024]{1,0:T(8,128)(2,1)S(1)} %pad_maximum_fusion.x_ref, f32[512,1024]{1,0:T(8,128)S(1)} %get-tuple-element.63.num_ref, f32[512,128]{1,0:T(8,128)S(1)} %get-tuple-element.64.den_ref, bf16[4,1024,1024]{2,1,0:T(8,128)(2,1)S(1)} %bitcast.30, f32[2,1024]{1,0:T(2,128)S(1)} %bitcast.51, ...), custom_call_target="tpu_custom_call" | custom-call | flops 1048576 | bytes 65536 | tf_op jit(solution)/shard_map/finish_part/pallas_call | solution.py:254
  (31 shorter events, 0.1 us)
Async XLA Ops:
  1.7 8.9 %collective-permute-start.2 = (f32[1,1024]{1,0:T(1,128)}, f32[1,1024]{1,0:T(1,128)S(1)}, u32[]{:S(2)}, u32[]{:S(2)}) collective-permute-start(f32[1,1024]{1,0:T(1,128)} %param.13), channel_id=1, source_target_pairs={{0,4},{4,0},{8,12},{12,8},{16,20},{20,16},{24,28},{28,24},{1,5},{5... | collective-permute-start | bytes 12296 | tf_op jit(solution)/shard_map/ppermute | solution.py:338
  1.8 9.6 %collective-permute-start = (f32[1,1024]{1,0:T(1,128)}, f32[1,1024]{1,0:T(1,128)S(1)}, u32[]{:S(2)}, u32[]{:S(2)}) collective-permute-start(f32[1,1024]{1,0:T(1,128)} %param.13), channel_id=1, source_target_pairs={{0,8},{4,12},{8,0},{12,4},{16,24},{20,28},{24,16},{28,20},{1,9},{5... | collective-permute-start | bytes 12296 | tf_op jit(solution)/shard_map/ppermute | solution.py:338
  3.4 8.0 %collective-permute-start.1 = (f32[1,1024]{1,0:T(1,128)}, f32[1,1024]{1,0:T(1,128)S(1)}, u32[]{:S(2)}, u32[]{:S(2)}) collective-permute-start(f32[1,1024]{1,0:T(1,128)} %param.13), channel_id=1, source_target_pairs={{0,12},{4,8},{8,4},{12,0},{16,28},{20,24},{24,20},{28,16},{1,13},{... | collective-permute-start | bytes 12296 | tf_op jit(solution)/shard_map/ppermute | solution.py:338
  3.7 27.5 %collective-permute-start.4 = (bf16[512,1024]{1,0:T(8,128)(2,1)}, bf16[512,1024]{1,0:T(8,128)(2,1)S(1)}, u32[]{:S(2)}, u32[]{:S(2)}) collective-permute-start(bf16[512,1024]{1,0:T(8,128)(2,1)} %bitcast.1.x_ref), channel_id=1, source_target_pairs={{0,1},{1,2},{2,3},{4,5},{5,6},{6,7},{8,9},{9,10},{10,11},{12,13},{... | collective-permute-start | bytes 3145736 | tf_op jit(solution)/shard_map/ppermute | solution.py:334
  8.3 22.6 %collective-permute-start.3 = (bf16[256,1024]{1,0:T(8,128)(2,1)S(1)}, bf16[256,1024]{1,0:T(8,128)(2,1)S(1)}, u32[]{:S(2)}, u32[]{:S(2)}) collective-permute-start(bf16[256,1024]{1,0:T(8,128)(2,1)S(1)} %slice_bitcast_fusion), channel_id=1, source_target_pairs={{1,0},{2,1},{3,2},{5,4},{6,5},{7,6},{9,8},{10,9},{11,10},{13,12},{... | collective-permute-start | bytes 1572872 | tf_op jit(solution)/shard_map/ppermute | solution.py:334
  11.4 3.4 %copy-start = (bf16[1,1,4,1024,1024]{4,3,2,1,0:T(8,128)(2,1)S(1)}, bf16[1,1,4,1024,1024]{4,3,2,1,0:T(8,128)(2,1)}, u32[]{:S(2)}) copy-start(bf16[1,1,4,1024,1024]{4,3,2,1,0:T(8,128)(2,1)} %param.9) | copy-start | bytes 25165828
  14.8 0.7 copy-start.2
  15.5 0.7 copy-start.4
  16.2 15.0 %copy-start.1 = (bf16[1,1,4,1024,1024]{4,3,2,1,0:T(8,128)(2,1)S(1)}, bf16[1,1,4,1024,1024]{4,3,2,1,0:T(8,128)(2,1)}, u32[]{:S(2)}) copy-start(bf16[1,1,4,1024,1024]{4,3,2,1,0:T(8,128)(2,1)} %param.9) | copy-start | bytes 25165828
  16.2 15.0 %copy-start.5 = (f32[1,1,2,1024]{3,2,1,0:T(2,128)S(1)}, f32[1,1,2,1024]{3,2,1,0:T(2,128)}, u32[]{:S(2)}) copy-start(f32[1,1,2,1024]{3,2,1,0:T(2,128)} %param.12) | copy-start | bytes 24580
  29.5 38.8 %collective-permute-start.6 = (bf16[512,1024]{1,0:T(8,128)(2,1)}, bf16[512,1024]{1,0:T(8,128)(2,1)S(1)}, u32[]{:S(2)}, u32[]{:S(2)}) collective-permute-start(bf16[512,1024]{1,0:T(8,128)(2,1)} %bitcast.1.x_ref), channel_id=1, source_target_pairs={{4,0},{8,4},{12,8},{16,12},{20,16},{24,20},{28,24},{5,1},{9,5},{13... | collective-permute-start | bytes 3145736 | tf_op jit(solution)/shard_map/ppermute | solution.py:334
  31.2 27.8 %slice-start = ((s8[8388608]{0:T(1024)(128)(4,1)}), s8[4194304]{0:T(1024)(128)(4,1)S(1)}, s32[]{:S(2)}) async-start(s8[8388608]{0:T(1024)(128)(4,1)} %bitcast.31), calls=%async_computation | async-start | bytes 8388608
  31.2 27.8 %slice-start.2 = ((s8[8388608]{0:T(1024)(128)(4,1)}), s8[4194304]{0:T(1024)(128)(4,1)S(1)}, s32[]{:S(2)}) async-start(s8[8388608]{0:T(1024)(128)(4,1)} %bitcast.36), calls=%async_computation.2 | async-start | bytes 8388608
  32.0 26.0 %collective-permute-start.5 = (bf16[256,1152]{1,0:T(8,128)(2,1)S(1)}, bf16[256,1152]{1,0:T(8,128)(2,1)S(1)}, u32[]{:S(2)}, u32[]{:S(2)}) collective-permute-start(bf16[256,1152]{1,0:T(8,128)(2,1)S(1)} %message_part.2), channel_id=1, source_target_pairs={{0,1},{1,2},{2,3},{4,5},{5,6},{6,7},{8,9},{9,10},{10,11},{12,13},{... | collective-permute-start | bytes 1769480 | tf_op jit(solution)/shard_map/ppermute | solution.py:334
  44.6 14.5 %slice-start.1 = ((s8[8388608]{0:T(1024)(128)(4,1)}), s8[4194304]{0:T(1024)(128)(4,1)S(1)}, s32[]{:S(2)}) async-start(s8[8388608]{0:T(1024)(128)(4,1)} %bitcast.31), calls=%async_computation.1 | async-start | bytes 8388608
  44.6 14.4 %slice-start.3 = ((s8[8388608]{0:T(1024)(128)(4,1)}), s8[4194304]{0:T(1024)(128)(4,1)S(1)}, s32[]{:S(2)}) async-start(s8[8388608]{0:T(1024)(128)(4,1)} %bitcast.36), calls=%async_computation.3 | async-start | bytes 8388608
  68.5 1.6 collective-permute-start.7
  70.3 10.9 %collective-permute-start.8 = (bf16[128,1024]{1,0:T(8,128)(2,1)S(1)}, bf16[128,1024]{1,0:T(8,128)(2,1)S(1)}, u32[]{:S(2)}, u32[]{:S(2)}) collective-permute-start(bf16[128,1024]{1,0:T(8,128)(2,1)S(1)} %get-tuple-element.68), channel_id=1, source_target_pairs={{0,8},{4,12},{8,0},{12,4},{16,24},{20,28},{24,16},{28,20},{1,9},{5... | collective-permute-start | bytes 786440 | tf_op jit(solution)/shard_map/ppermute | solution.py:338
  81.6 1.7 %collective-permute-start.10 = (bf16[128,1024]{1,0:T(8,128)(2,1)S(1)}, bf16[128,1024]{1,0:T(8,128)(2,1)S(1)}, u32[]{:S(2)}, u32[]{:S(2)}) collective-permute-start(bf16[128,1024]{1,0:T(8,128)(2,1)S(1)} %select_convert_fusion.2), channel_id=1, source_target_pairs={{0,4},{4,0},{8,12},{12,8},{16,20},{20,16},{24,28},{28,24},{1,5},{5... | collective-permute-start | bytes 786440 | tf_op jit(solution)/shard_map/ppermute | solution.py:338
  81.7 8.7 %collective-permute-start.9 = (bf16[128,1024]{1,0:T(8,128)(2,1)S(1)}, bf16[128,1024]{1,0:T(8,128)(2,1)S(1)}, u32[]{:S(2)}, u32[]{:S(2)}) collective-permute-start(bf16[128,1024]{1,0:T(8,128)(2,1)S(1)} %fusion.5), channel_id=1, source_target_pairs={{0,16},{4,20},{8,24},{12,28},{16,0},{20,4},{24,8},{28,12},{1,17},{... | collective-permute-start | bytes 786440 | tf_op jit(solution)/shard_map/ppermute | solution.py:338
  83.6 8.4 %collective-permute-start.12 = (bf16[128,1024]{1,0:T(8,128)(2,1)S(1)}, bf16[128,1024]{1,0:T(8,128)(2,1)S(1)}, u32[]{:S(2)}, u32[]{:S(2)}) collective-permute-start(bf16[128,1024]{1,0:T(8,128)(2,1)S(1)} %get-tuple-element.65), channel_id=1, source_target_pairs={{0,8},{4,12},{8,0},{12,4},{16,24},{20,28},{24,16},{28,20},{1,9},{5... | collective-permute-start | bytes 786440 | tf_op jit(solution)/shard_map/ppermute | solution.py:338
  90.6 1.6 collective-permute-start.11
  93.7 8.4 %collective-permute-start.13 = (bf16[128,1024]{1,0:T(8,128)(2,1)S(1)}, bf16[128,1024]{1,0:T(8,128)(2,1)S(1)}, u32[]{:S(2)}, u32[]{:S(2)}) collective-permute-start(bf16[128,1024]{1,0:T(8,128)(2,1)S(1)} %fusion.8), channel_id=1, source_target_pairs={{0,16},{4,20},{8,24},{12,28},{16,0},{20,4},{24,8},{28,12},{1,17},{... | collective-permute-start | bytes 786440 | tf_op jit(solution)/shard_map/ppermute | solution.py:338
  95.4 15.7 %collective-permute-start.15 = (bf16[256,1024]{1,0:T(8,128)(2,1)S(1)}, bf16[256,1024]{1,0:T(8,128)(2,1)S(1)}, u32[]{:S(2)}, u32[]{:S(2)}) collective-permute-start(bf16[256,1024]{1,0:T(8,128)(2,1)S(1)} %fusion), channel_id=1, source_target_pairs={{0,1},{1,2},{2,3},{4,5},{5,6},{6,7},{8,9},{9,10},{10,11},{12,13},{... | collective-permute-start | bytes 1572872 | tf_op jit(solution)/shard_map/ppermute | solution.py:334
  102.3 2.0 %collective-permute-start.14 = (bf16[128,1024]{1,0:T(8,128)(2,1)S(1)}, bf16[128,1024]{1,0:T(8,128)(2,1)S(1)}, u32[]{:S(2)}, u32[]{:S(2)}) collective-permute-start(bf16[128,1024]{1,0:T(8,128)(2,1)S(1)} %select_convert_fusion), channel_id=1, source_target_pairs={{0,4},{4,0},{8,12},{12,8},{16,20},{20,16},{24,28},{28,24},{1,5},{5... | collective-permute-start | bytes 786440 | tf_op jit(solution)/shard_map/ppermute | solution.py:338
  102.4 27.1 %collective-permute-start.16 = (bf16[256,1024]{1,0:T(8,128)(2,1)S(1)}, bf16[256,1024]{1,0:T(8,128)(2,1)S(1)}, u32[]{:S(2)}, u32[]{:S(2)}) collective-permute-start(bf16[256,1024]{1,0:T(8,128)(2,1)S(1)} %fusion), channel_id=1, source_target_pairs={{1,0},{2,1},{3,2},{5,4},{6,5},{7,6},{9,8},{10,9},{11,10},{13,12},{... | collective-permute-start | bytes 1572872 | tf_op jit(solution)/shard_map/ppermute | solution.py:334
  111.3 5.7 %copy-start.3 = (s32[1,2048]{1,0:T(1,128)S(1)}, s32[1,2048]{1,0:T(1,128)}, u32[]{:S(2)}) copy-start(s32[1,2048]{1,0:T(1,128)} %doc_ref.15) | copy-start | bytes 24580
  112.5 17.1 %collective-permute-start.17 = (bf16[256,1024]{1,0:T(8,128)(2,1)S(1)}, bf16[256,1024]{1,0:T(8,128)(2,1)S(1)}, u32[]{:S(2)}, u32[]{:S(2)}) collective-permute-start(bf16[256,1024]{1,0:T(8,128)(2,1)S(1)} %fusion.1), channel_id=1, source_target_pairs={{0,1},{1,2},{2,3},{4,5},{5,6},{6,7},{8,9},{9,10},{10,11},{12,13},{... | collective-permute-start | bytes 1572872 | tf_op jit(solution)/shard_map/ppermute | solution.py:334
  130.7 22.8 %collective-permute-start.18 = (bf16[256,1152]{1,0:T(8,128)(2,1)S(1)}, bf16[256,1152]{1,0:T(8,128)(2,1)S(1)}, u32[]{:S(2)}, u32[]{:S(2)}) collective-permute-start(bf16[256,1152]{1,0:T(8,128)(2,1)S(1)} %message_part.3), channel_id=1, source_target_pairs={{0,1},{1,2},{2,3},{4,5},{5,6},{6,7},{8,9},{9,10},{10,11},{12,13},{... | collective-permute-start | bytes 1769480 | tf_op jit(solution)/shard_map/ppermute | solution.py:334
where the time goes:
time: 168 us; the launch traced here: 169 us
  Pallas kernels  75.8 us (45%)
  starting transfers between devices  49.2 us (29%)
  waiting for transfers between devices  31 us (18%)
  local copies, waits for them, and re-layouts  7.69 us (5%)
  other arithmetic  5.13 us (3%)
    pallas_call x11, Pallas kernels, call(): pl.pallas_call(kernel, in_specs=in_specs, out_specs=[vmem()] * len(result...  75.8 us
    ppermute x8, starting transfers between devices, shifted(): lax.ppermute(value, axis, [(i, i + steps) for i in range(first, last)])  41.7 us
    ppermute x8, waiting for transfers between devices, shifted(): lax.ppermute(value, axis, [(i, i + steps) for i in range(first, last)])  19.3 us
    ppermute x11, waiting for transfers between devices, swapped(): lax.ppermute(value, axis, [(i, i ^ bit) for i in range(lax.axis_size(axis...  11.6 us
    ppermute x11, starting transfers between devices, swapped(): lax.ppermute(value, axis, [(i, i ^ bit) for i in range(lax.axis_size(axis...  7.52 us
    unnamed x21, local copies, waits for them, and re-layouts  4.84 us
  transfers between devices with their start and end apart: 19, of which 9 were waited for; matrix products, arithmetic and copies ran while one was open for 2% of the time, Pallas kernels for 35%

commit v1 on v0

--- a/solution.py
+++ b/solution.py
@@ -11,7 +11,7 @@
 LANES = 128
 BLOCK = 256
 TILE = 512
-TILES = 2
+TILES = 8
 VMEM_BYTES = 12 * 1024 * 1024
 COST = pl.CostEstimate(flops=1 << 20, bytes_accessed=1 << 16, transcendentals=0)
 F32 = jnp.float32
@@ -80,7 +80,7 @@
                 return den
 
             den = jnp.zeros((q_block, LANES), F32)
-            den_ref[pl.ds(q0, q_block), :] += lax.fori_loop(0, width // LANES // TILES, some, den)
+            den_ref[pl.ds(q0, q_block), :] += lax.fori_loop(0, width // LANES // TILES, some, den, unroll=True)
 
         return carry
 
@@ -99,48 +99,49 @@
     return rms_norm(x_ref[...].astype(F32), gain_ref[0:1]).astype(BF16)
 
 
-def project(n_ref, w_ref, index, out_ref, scale=None):
-    width = w_ref.shape[2]
+def project(n_ref, w_ref, first, out_ref):
+    count, _, width = out_ref.shape
     tile = min(TILE, width)
-
-    def one(j, carry):
+    steps = width // tile
+
+    def one(step, carry):
+        i, j = step // steps, step % steps
         cols = pl.ds(pl.multiple_of(j * tile, tile), tile)
-        out = dot(n_ref[...], w_ref[index, :, cols]).astype(BF16)
-        out_ref[:, cols] = out if scale is None else out * jnp.asarray(scale, BF16)
+        out = dot(n_ref[...], w_ref[first + i, :, cols]).astype(BF16)
+        if first == 0:
+            out *= jnp.where(i == 0, (width // HEADS) ** (-0.5), 1.0).astype(BF16)
+        out_ref[i, :, cols] = out
         return carry
 
-    lax.fori_loop(0, width // tile, one, 0)
-
-
-def own_kernel(
-    x_ref, gain_ref, w_ref, column_ref, row_ref, doc_ref, q_ref, num_ref, den_ref, n_ref, k_ref, v_ref
-):
-    head_dim = x_ref.shape[1] // HEADS
+    lax.fori_loop(0, count * steps, one, 0)
+
+
+def own_kernel(x_ref, gain_ref, w_ref, column_ref, row_ref, doc_ref, qkv_ref, num_ref, den_ref, n_ref):
     here = lax.axis_index("seq") * x_ref.shape[0]
     n_ref[...] = normed(x_ref, gain_ref)
-    project(n_ref, w_ref, 0, q_ref, head_dim ** (-0.5))
-    project(n_ref, w_ref, 1, k_ref)
-    project(n_ref, w_ref, 2, v_ref)
+    project(n_ref, w_ref, 0, qkv_ref)
     num_ref[...] = jnp.zeros_like(num_ref)
     den_ref[...] = jnp.zeros_like(den_ref)
+    q_ref, k_ref, v_ref = [qkv_ref.at[i] for i in range(3)]
     attend(q_ref, k_ref, v_ref, num_ref, den_ref, column_ref, row_ref, doc_ref, here, here, True)
 
 
 def piece_kernel(
-    shift, first, x_ref, gain_ref, w_ref, q_ref, num_in, den_in, column_ref, row_ref, doc_ref,
-    num_ref, den_ref, n_ref, k_ref, v_ref,
+    shift, first, x_ref, gain_ref, w_ref, qkv_ref, num_in, den_in, column_ref, row_ref, doc_ref,
+    num_ref, den_ref, n_ref, kv_ref,
 ):
     del num_in, den_in
-    rows, keys = q_ref.shape[0], x_ref.shape[0]
+    rows, keys = qkv_ref.shape[1], x_ref.shape[0]
     shard = lax.axis_index("seq") - shift
     here, there = (shard + shift) * rows, jnp.maximum(shard, 0) * rows + first
 
     @pl.when((shard >= 0) & (doc_ref[0, there + keys - 1] >= doc_ref[0, here]))
     def _():
         n_ref[...] = normed(x_ref, gain_ref)
-        project(n_ref, w_ref, 1, k_ref)
-        project(n_ref, w_ref, 2, v_ref)
-        attend(q_ref, k_ref, v_ref, num_ref, den_ref, column_ref, row_ref, doc_ref, here, there)
+        project(n_ref, w_ref, 1, kv_ref)
+        attend(
+            qkv_ref.at[0], kv_ref.at[0], kv_ref.at[1], num_ref, den_ref, column_ref, row_ref, doc_ref, here, there
+        )
 
 
 def far_document(doc_ref, rows, count):
@@ -154,7 +155,7 @@
 
 def message_kernel(
     x_ref, piece_ref, gain_ref, w_ref, column_ref, row_ref, doc_ref,
-    out_ref, q_ref, n_ref, k_ref, v_ref, num_ref, den_ref,
+    out_ref, q_ref, n_ref, kv_ref, num_ref, den_ref,
 ):
     half, width = x_ref.shape
     rows = 2 * half
@@ -177,21 +178,22 @@
         @pl.when(inside & (doc_ref[0, there + rows - 1] >= doc_ref[0, here]))
         def _():
             n_ref[:half] = normed(x_ref, gain_ref)
-            project(n_ref.at[:half], w_ref, 0, q_ref, (width // HEADS) ** (-0.5))
+            project(n_ref.at[:half], w_ref, 0, q_ref)
             n_ref[...] = normed(piece_ref, gain_ref)
-            project(n_ref, w_ref, 1, k_ref)
-            project(n_ref, w_ref, 2, v_ref)
-            attend(q_ref, k_ref, v_ref, num_ref, den_ref, column_ref, row_ref, doc_ref, here, there)
+            project(n_ref, w_ref, 1, kv_ref)
+            attend(
+                q_ref.at[0], kv_ref.at[0], kv_ref.at[1], num_ref, den_ref, column_ref, row_ref, doc_ref, here, there
+            )
 
         out_ref[:, :width] = num_ref[...].astype(BF16)
         out_ref[:, width:] = den_ref[...].astype(BF16)
 
 
 def reply_kernel(
-    message_ref, gain_ref, w_ref, q_ref, num_in, den_in, column_ref, row_ref, doc_ref,
-    num_ref, den_ref, n_ref, k_ref, v_ref,
+    message_ref, gain_ref, w_ref, qkv_ref, num_in, den_in, column_ref, row_ref, doc_ref,
+    num_ref, den_ref, n_ref, kv_ref,
 ):
-    rows, width = q_ref.shape
+    _, rows, width = qkv_ref.shape
     half = message_ref.shape[0]
     far = far_document(doc_ref, rows, lax.axis_size("seq"))
 
@@ -203,8 +205,8 @@
     @pl.when(jnp.logical_not(far))
     def _():
         piece_kernel(
-            2, half, message_ref.at[:, :width], gain_ref, w_ref, q_ref, num_in, den_in, column_ref, row_ref, doc_ref,
-            num_ref, den_ref, n_ref, k_ref, v_ref,
+            2, half, message_ref.at[:, :width], gain_ref, w_ref, qkv_ref, num_in, den_in, column_ref, row_ref, doc_ref,
+            num_ref, den_ref, n_ref, kv_ref,
         )
 
 
@@ -231,9 +233,8 @@
     hidden_ref[0] = expand(0)
 
     def one(j, carry):
-        expanded = expand(j + 1)
         acc_ref[...] += lower(j, hidden_ref[j % 2])
-        hidden_ref[(j + 1) % 2] = expanded
+        hidden_ref[(j + 1) % 2] = expand(j + 1)
         return carry
 
     last = hidden // tile - 1
@@ -266,20 +267,21 @@
 
 def own_part(x, gains, weights, docs):
     rows, width = x.shape
-    results = [((rows, width), BF16), ((rows, width), F32), ((rows, LANES), F32)]
-    scratch = [pltpu.VMEM((rows, width), BF16)] * 3
+    results = [((3, rows, width), BF16), ((rows, width), F32), ((rows, LANES), F32)]
+    scratch = [pltpu.VMEM((rows, width), BF16)]
     return call(own_kernel, "own_part", (x, gains, weights[0], docs.own_column, docs.ids), docs.ids, results, scratch)
 
 
-def piece_part(x, shift, gains, w_attn, q, num, den, docs):
-    rows, width = q.shape
+def piece_part(x, shift, gains, w_attn, qkv, num, den, docs):
+    _, rows, width = qkv.shape
+    keys = x.shape[0]
     return call(
         functools.partial(piece_kernel, shift, 0),
         "piece_part",
-        (x, gains, w_attn, q, num, den, docs.own_column, docs.ids),
+        (x, gains, w_attn, qkv, num, den, docs.own_column, docs.ids),
         docs.ids,
         [((rows, width), F32), ((rows, LANES), F32)],
-        [pltpu.VMEM((x.shape[0], width), BF16)] * 3,
+        [pltpu.VMEM((keys, width), BF16), pltpu.VMEM((2, keys, width), BF16)],
         aliases={4: 0, 5: 1},
     )
 
@@ -293,21 +295,21 @@
         (x, piece, gains, w_attn, docs.later_column, docs.ids),
         docs.ids,
         [((half, width + LANES), BF16)],
-        [pltpu.VMEM((half, width), BF16)]
-        + [pltpu.VMEM((keys, width), BF16)] * 3
+        [pltpu.VMEM((1, half, width), BF16), pltpu.VMEM((keys, width), BF16), pltpu.VMEM((2, keys, width), BF16)]
         + [pltpu.VMEM((half, width), F32), pltpu.VMEM((half, LANES), F32)],
     )[0]
 
 
-def reply_part(message, gains, w_attn, q, num, den, docs):
-    rows, width = q.shape
+def reply_part(message, gains, w_attn, qkv, num, den, docs):
+    _, rows, width = qkv.shape
+    keys = message.shape[0]
     return call(
         reply_kernel,
         "reply_part",
-        (message, gains, w_attn, q, num, den, docs.own_column, docs.ids),
+        (message, gains, w_attn, qkv, num, den, docs.own_column, docs.ids),
         docs.ids,
         [((rows, width), F32), ((rows, LANES), F32)],
-        [pltpu.VMEM((message.shape[0], width), BF16)] * 3,
+        [pltpu.VMEM((keys, width), BF16), pltpu.VMEM((2, keys, width), BF16)],
         aliases={4: 0, 5: 1},
     )
 
@@ -330,8 +332,11 @@
 
 def shifted(value, axis, steps):
     count = lax.axis_size(axis)
-    first, last = max(0, -steps), min(count, count - steps)
-    return lax.ppermute(value, axis, [(i, i + steps) for i in range(first, last)])
+    return lax.ppermute(value, axis, [(i, (i + steps) % count) for i in range(count)])
+
+
+def sent_back(value, axis):
+    return lax.ppermute(value, axis, [(i, i - 1) for i in range(1, lax.axis_size(axis))])
 
 
 def swapped(value, axis, bit):
@@ -356,17 +361,21 @@
         self.later_column = column(1, self.half) if self.short else self.own_column
 
 
-def attention(state, piece, first_back, docs, gains, w_attn):
-    q, *state = state
+def attention(state, piece, first_back, docs, gains, w_attn, meanwhile=lambda token: ()):
+    qkv, *state = state
     if docs.short:
-        message = shifted(message_part(after(first_back, q), piece, gains, w_attn, docs), "seq", 1)
-        num, den = piece_part(piece, 1, gains, w_attn, q, *state, docs)
-        return reply_part(message, gains, w_attn, q, num, den, docs)
-    state = piece_part(piece, 1, gains, w_attn, q, *state, docs)
+        message = message_part(after(first_back, qkv), piece, gains, w_attn, docs)
+        message = shifted(message, "seq", 1)
+        num, den = piece_part(piece, 1, gains, w_attn, qkv, *state, docs)
+        done = meanwhile(den)
+        num = after(num, *jax.tree.leaves(done))
+        return reply_part(message, gains, w_attn, qkv, num, den, docs), done
+    state = piece_part(piece, 1, gains, w_attn, qkv, *state, docs)
+    done = meanwhile(state[1])
     for hop in range(2, docs.hops + 1):
         piece = shifted(piece, "seq", 1)
-        state = piece_part(piece, hop, gains, w_attn, q, *state, docs)
-    return state
+        state = piece_part(piece, hop, gains, w_attn, qkv, *state, docs)
+    return state, done
 
 
 def gain_factors(gain, bits):
@@ -438,7 +447,7 @@
     weights = (w_attn[0, 0], w_up[0, 0], w_down[0, 0])
     parts = [x[:half], x[half:]]
     piece = shifted(x, "seq", 1)
-    first_back = shifted(parts[0], "seq", -1)
+    first_back = sent_back(parts[0], "seq")
     docs = Documents(doc_ids, rows)
     place, bits, bit = lax.axis_index("depth"), {}, 1
     while bit < lax.axis_size("depth"):
@@ -447,10 +456,11 @@
     early, bits, docs.own_column, docs.later_column = lax.optimization_barrier(
         (x, bits, docs.own_column, docs.later_column)
     )
-    factors = gain_factors(after(coarse_gain, docs.own_column), bits)
-    state = own_part(after(early, *jax.tree.leaves(factors)), gains, weights, docs)
-    following = shifted(after(x, state[0]), "depth", -1)
-    num, den = attention(state, piece, first_back, docs, gains, weights[0])
+    state = own_part(early, gains, weights, docs)
+    following = sent_back(after(x, state[0]), "depth")
+    (num, den), factors = attention(
+        state, piece, first_back, docs, gains, weights[0], lambda token: gain_factors(after(coarse_gain, token), bits)
+    )
     following = [following[:half], following[half:]]
     first, second = [Chain(parts[i], following[i], factors, bits) for i in range(2)]
     first.enter(finish_part(x, num, den, weights, gains, 0, 2))
@@ -462,14 +472,14 @@
         first.level(i, used_after=(second.entered,))
     corrected = [first.leave()]
     halves = [shifted(corrected[0], "seq", 1)]
-    first_back = shifted(corrected[0], "seq", -1)
+    first_back = sent_back(corrected[0], "seq")
     second.level(len(first.levels) - 1, sent_after=(corrected[0],))
     corrected.append(second.leave(used_after=(halves[0],)))
     halves.append(shifted(corrected[1], "seq", 1))
     x = jnp.concatenate(corrected, axis=0)
     state = own_part(x, gains, weights, docs)
     piece = jnp.concatenate(halves, axis=0)
-    num, den = attention(state, piece, first_back, docs, gains, weights[0])
+    (num, den), _ = attention(state, piece, first_back, docs, gains, weights[0])
     return finish_part(x, num, den, weights, gains, 0, 1)[None, None]
 
 

time: 168 us -> 166 us (0.988)
  the two profiles are of different devices: /device:TPU:8 before, /device:TPU:0 now
where the time goes in v1:
time: 166 us; the launch traced here: 165 us
  waiting for transfers between devices  76.9 us (46%)
  Pallas kernels  57.5 us (35%)
  starting transfers between devices  15.4 us (9%)
  local copies, waits for them, and re-layouts  9.93 us (6%)
  other arithmetic  4.43 us (3%)
    pallas_call x11, Pallas kernels, call(): pl.pallas_call(kernel, in_specs=in_specs, out_specs=[vmem()] * len(result...  57.5 us
    ppermute x5, waiting for transfers between devices, shifted(): lax.ppermute(value, axis, [(i, (i + steps) % count) for i in range(count)])  42.2 us
    ppermute x11, waiting for transfers between devices, swapped(): lax.ppermute(value, axis, [(i, i ^ bit) for i in range(lax.axis_size(axis...  18.7 us
    ppermute x3, waiting for transfers between devices, sent_back(): lax.ppermute(value, axis, [(i, i - 1) for i in range(1, lax.axis_size(axi...  15.9 us
    ppermute x11, starting transfers between devices, swapped(): lax.ppermute(value, axis, [(i, i ^ bit) for i in range(lax.axis_size(axis...  7.81 us
    unnamed x27, local copies, waits for them, and re-layouts  7.05 us
    ppermute x3, starting transfers between devices, sent_back(): lax.ppermute(value, axis, [(i, i - 1) for i in range(1, lax.axis_size(axi...  3.88 us
    ppermute x5, starting transfers between devices, shifted(): lax.ppermute(value, axis, [(i, (i + steps) % count) for i in range(count)])  3.71 us
  transfers between devices with their start and end apart: 19, of which 13 were waited for; matrix products, arithmetic and copies ran while one was open for 3% of the time, Pallas kernels for 25%

profile of v1, /device:TPU:0, one launch (start us, length us, event | category | flops | bytes accessed | tf_op | source)
XLA Modules:
  0.0 164.6 jit_solution(6389201350481796096)
XLA Ops:
  0.0 3.0 %collective-permute-start = (bf16[512,1024]{1,0:T(8,128)(2,1)}, bf16[512,1024]{1,0:T(8,128)(2,1)S(1)}, u32[]{:S(2)}, u32[]{:S(2)}) collective-permute-start(bf16[512,1024]{1,0:T(8,128)(2,1)} %bitcast.1.x_ref), channel_id=1, source_target_pairs={{0,1},{1,2},{2,3},{3,0},{4,5},{5,6},{6,7},{7,4},{8,9},{9,10},{10,1... | collective-permute-start | bytes 3145736 | tf_op jit(solution)/shard_map/ppermute | solution.py:335
  3.0 1.1 slice_bitcast_fusion
  4.1 1.3 collective-permute-start.4
  5.5 0.8 constant_dynamic-slice_fusion.1
  6.2 0.8 constant_dynamic-slice_fusion
  7.0 0.1 broadcast_in_dim.21.column_ref
  7.1 0.1 broadcast_in_dim.23.column_ref
  7.2 3.4 %copy-done = bf16[1,1,4,1024,1024]{4,3,2,1,0:T(8,128)(2,1)S(1)} copy-done((bf16[1,1,4,1024,1024]{4,3,2,1,0:T(8,128)(2,1)S(1)}, bf16[1,1,4,1024,1024]{4,3,2,1,0:T(8,128)(2,1)}, u32[]{:S(2)}) %copy-start) | copy-done | bytes 8388632
  10.6 0.7 copy-done.4
  11.3 0.7 copy-done.6
  12.0 10.5 %own_part.2 = (bf16[3,512,1024]{2,1,0:T(8,128)(2,1)S(1)}, f32[512,1024]{1,0:T(8,128)S(1)}, f32[512,128]{1,0:T(8,128)S(1)}) custom-call(bf16[512,1024]{1,0:T(8,128)(2,1)} %bitcast.1.x_ref, f32[2,1024]{1,0:T(2,128)S(1)} %bitcast.41, bf16[4,1024,1024]{2,1,0:T(8,128)(2,1)S(1)} %bitcast.20, s32[512,128]{1,0:T(8,128)S(1)} %broadcast_in_dim.21.column_ref, ...), custom_call_target="tpu_custom_call" | custom-call | flops 1048576 | bytes 65536 | tf_op jit(solution)/shard_map/own_part/pallas_call | solution.py:255
  22.5 1.3 collective-permute-start.6
  23.8 15.9 %collective-permute-done.4.x_ref = bf16[256,1024]{1,0:T(8,128)(2,1)S(1)} collective-permute-done((bf16[256,1024]{1,0:T(8,128)(2,1)S(1)}, bf16[256,1024]{1,0:T(8,128)(2,1)S(1)}, u32[]{:S(2)}, u32[]{:S(2)}) %collective-permute-start.4) | collective-permute-done | bytes 524320 | tf_op jit(solution)/shard_map/ppermute | solution.py:339
  39.7 0.7 message_part.2
  40.4 0.2 copy-done.2
  40.6 0.6 collective-permute-start.5
  41.2 2.0 %copy-done.3 = bf16[512,1024]{1,0:T(8,128)(2,1)S(1)} copy-done((bf16[512,1024]{1,0:T(8,128)(2,1)S(1)}, bf16[512,1024]{1,0:T(8,128)(2,1)}, u32[]{:S(2)}) %copy-start.3) | copy-done | bytes 1048600
  43.2 0.7 piece_part.2
  43.9 1.6 collective-permute-start.1
  45.5 0.6 collective-permute-start.3
  46.1 1.5 collective-permute-done.1
  47.6 0.9 collective-permute-done.2
  48.5 9.1 %collective-permute-done.5.message_ref = bf16[256,1152]{1,0:T(8,128)(2,1)S(1)} collective-permute-done((bf16[256,1152]{1,0:T(8,128)(2,1)S(1)}, bf16[256,1152]{1,0:T(8,128)(2,1)S(1)}, u32[]{:S(2)}, u32[]{:S(2)}) %collective-permute-start.5) | collective-permute-done | bytes 589856 | tf_op jit(solution)/shard_map/ppermute | solution.py:335
  57.7 0.9 reply_part.2
  58.6 9.0 %finish_part.3 = bf16[256,1024]{1,0:T(8,128)(2,1)S(1)} custom-call(bf16[512,1024]{1,0:T(8,128)(2,1)} %bitcast.1.x_ref, f32[512,1024]{1,0:T(8,128)S(1)} %get-tuple-element.52.num_ref, f32[512,128]{1,0:T(8,128)S(1)} %get-tuple-element.50.den_ref, bf16[4,1024,1024]{2,1,0:T(8,128)(2,1)S(1)} %bitcast.24, f32[2,1024]{1,0:T(2,128)S(1)} %bitcast.45, ...), custom_call_target="tpu_custom_call" | custom-call | flops 1048576 | bytes 65536 | tf_op jit(solution)/shard_map/finish_part/pallas_call | solution.py:255
  67.6 0.2 convert_subtract_fusion.1
  67.9 0.1 collective-permute-start.7
  67.9 1.5 collective-permute-done.7
  69.5 0.2 fusion.13
  69.6 1.6 collective-permute-start.8
  71.2 9.0 %finish_part.4 = bf16[256,1024]{1,0:T(8,128)(2,1)S(1)} custom-call(bf16[512,1024]{1,0:T(8,128)(2,1)} %bitcast.1.x_ref, f32[512,1024]{1,0:T(8,128)S(1)} %get-tuple-element.52.num_ref, f32[512,128]{1,0:T(8,128)S(1)} %get-tuple-element.50.den_ref, bf16[4,1024,1024]{2,1,0:T(8,128)(2,1)S(1)} %bitcast.25, f32[2,1024]{1,0:T(2,128)S(1)} %bitcast.46, ...), custom_call_target="tpu_custom_call" | custom-call | flops 1048576 | bytes 65536 | tf_op jit(solution)/shard_map/finish_part/pallas_call | solution.py:255
  80.2 0.1 fusion.5
  80.3 0.2 convert_subtract_fusion
  80.5 0.1 collective-permute-start.10
  80.6 1.6 collective-permute-start.9
  82.2 0.1 fusion.11
  82.3 0.6 collective-permute-start.12
  82.9 6.4 %collective-permute-done.9 = bf16[128,1024]{1,0:T(8,128)(2,1)S(1)} collective-permute-done((bf16[128,1024]{1,0:T(8,128)(2,1)S(1)}, bf16[128,1024]{1,0:T(8,128)(2,1)S(1)}, u32[]{:S(2)}, u32[]{:S(2)}) %collective-permute-start.9) | collective-permute-done | bytes 262176 | tf_op jit(solution)/shard_map/ppermute | solution.py:343
  89.3 0.2 select_convert_fusion.1
  89.5 0.1 collective-permute-start.11
  89.6 1.2 collective-permute-done.12
  90.8 0.1 fusion.8
  90.9 0.2 collective-permute-done.11
  91.1 0.3 convert_select_fusion.5
  91.4 1.2 fusion
  92.6 1.6 collective-permute-start.13
  94.2 6.8 %collective-permute-done.13 = bf16[128,1024]{1,0:T(8,128)(2,1)S(1)} collective-permute-done((bf16[128,1024]{1,0:T(8,128)(2,1)S(1)}, bf16[128,1024]{1,0:T(8,128)(2,1)S(1)}, u32[]{:S(2)}, u32[]{:S(2)}) %collective-permute-start.13) | collective-permute-done | bytes 262176 | tf_op jit(solution)/shard_map/ppermute | solution.py:343
  101.0 0.2 select_convert_fusion
  101.2 0.1 collective-permute-start.14
  101.3 1.3 collective-permute-start.16
  102.6 0.2 collective-permute-done.14
  102.8 8.0 %collective-permute-done.15 = bf16[256,1024]{1,0:T(8,128)(2,1)S(1)} collective-permute-done((bf16[256,1024]{1,0:T(8,128)(2,1)S(1)}, bf16[256,1024]{1,0:T(8,128)(2,1)S(1)}, u32[]{:S(2)}, u32[]{:S(2)}) %collective-permute-start.15) | collective-permute-done | bytes 524320 | tf_op jit(solution)/shard_map/ppermute | solution.py:335
  110.8 0.3 convert_select_fusion.3
  111.1 1.2 fusion.1
  112.3 0.1 collective-permute-start.17
  112.4 0.1 pad_maximum_fusion.x_ref
  112.5 9.9 %own_part.3 = (bf16[3,512,1024]{2,1,0:T(8,128)(2,1)S(1)}, f32[512,1024]{1,0:T(8,128)S(1)}, f32[512,128]{1,0:T(8,128)S(1)}) custom-call(bf16[512,1024]{1,0:T(8,128)(2,1)S(1)} %pad_maximum_fusion.x_ref, f32[2,1024]{1,0:T(2,128)S(1)} %bitcast.47, bf16[4,1024,1024]{2,1,0:T(8,128)(2,1)S(1)} %bitcast.26, s32[512,128]{1,0:T(8,128)S(1)} %broadcast_in_dim.21.column_ref, ...), custom_call_target="tpu_custom_call" | custom-call | flops 1048576 | bytes 65536 | tf_op jit(solution)/shard_map/own_part/pallas_call | solution.py:255
  122.4 9.8 %collective-permute-done.17 = bf16[256,1024]{1,0:T(8,128)(2,1)S(1)} collective-permute-done((bf16[256,1024]{1,0:T(8,128)(2,1)S(1)}, bf16[256,1024]{1,0:T(8,128)(2,1)S(1)}, u32[]{:S(2)}, u32[]{:S(2)}) %collective-permute-start.17) | collective-permute-done | bytes 524320 | tf_op jit(solution)/shard_map/ppermute | solution.py:335
  132.3 0.9 message_part.3
  133.2 0.1 collective-permute-start.18
  133.3 0.7 piece_part.3
  134.0 15.3 %collective-permute-done.18.message_ref = bf16[256,1152]{1,0:T(8,128)(2,1)S(1)} collective-permute-done((bf16[256,1152]{1,0:T(8,128)(2,1)S(1)}, bf16[256,1152]{1,0:T(8,128)(2,1)S(1)}, u32[]{:S(2)}, u32[]{:S(2)}) %collective-permute-start.18) | collective-permute-done | bytes 589856 | tf_op jit(solution)/shard_map/ppermute | solution.py:335
  149.2 0.7 reply_part.3
  150.0 14.6 %finish_part.5 = bf16[512,1024]{1,0:T(8,128)(2,1)} custom-call(bf16[512,1024]{1,0:T(8,128)(2,1)S(1)} %pad_maximum_fusion.x_ref, f32[512,1024]{1,0:T(8,128)S(1)} %get-tuple-element.63.num_ref, f32[512,128]{1,0:T(8,128)S(1)} %get-tuple-element.64.den_ref, bf16[4,1024,1024]{2,1,0:T(8,128)(2,1)S(1)} %bitcast.30, f32[2,1024]{1,0:T(2,128)S(1)} %bitcast.51, ...), custom_call_target="tpu_custom_call" | custom-call | flops 1048576 | bytes 65536 | tf_op jit(solution)/shard_map/finish_part/pallas_call | solution.py:255
  (37 shorter events, 0.3 us)
Async XLA Ops:
  0.0 39.7 %collective-permute-start = (bf16[512,1024]{1,0:T(8,128)(2,1)}, bf16[512,1024]{1,0:T(8,128)(2,1)S(1)}, u32[]{:S(2)}, u32[]{:S(2)}) collective-permute-start(bf16[512,1024]{1,0:T(8,128)(2,1)} %bitcast.1.x_ref), channel_id=1, source_target_pairs={{0,1},{1,2},{2,3},{3,0},{4,5},{5,6},{6,7},{7,4},{8,9},{9,10},{10,1... | collective-permute-start | bytes 3145736 | tf_op jit(solution)/shard_map/ppermute | solution.py:335
  4.1 35.5 %collective-permute-start.4 = (bf16[256,1024]{1,0:T(8,128)(2,1)S(1)}, bf16[256,1024]{1,0:T(8,128)(2,1)S(1)}, u32[]{:S(2)}, u32[]{:S(2)}) collective-permute-start(bf16[256,1024]{1,0:T(8,128)(2,1)S(1)} %slice_bitcast_fusion), channel_id=1, source_target_pairs={{1,0},{2,1},{3,2},{5,4},{6,5},{7,6},{9,8},{10,9},{11,10},{13,12},{... | collective-permute-start | bytes 1572872 | tf_op jit(solution)/shard_map/ppermute | solution.py:339
  7.2 3.4 %copy-start = (bf16[1,1,4,1024,1024]{4,3,2,1,0:T(8,128)(2,1)S(1)}, bf16[1,1,4,1024,1024]{4,3,2,1,0:T(8,128)(2,1)}, u32[]{:S(2)}) copy-start(bf16[1,1,4,1024,1024]{4,3,2,1,0:T(8,128)(2,1)} %param.9) | copy-start | bytes 25165828
  10.6 0.7 copy-start.4
  11.3 0.7 copy-start.6
  12.0 27.7 %copy-start.1 = (bf16[1,1,4,1024,1024]{4,3,2,1,0:T(8,128)(2,1)S(1)}, bf16[1,1,4,1024,1024]{4,3,2,1,0:T(8,128)(2,1)}, u32[]{:S(2)}) copy-start(bf16[1,1,4,1024,1024]{4,3,2,1,0:T(8,128)(2,1)} %param.9) | copy-start | bytes 25165828
  12.0 27.7 %copy-start.7 = (f32[1,1,2,1024]{3,2,1,0:T(2,128)S(1)}, f32[1,1,2,1024]{3,2,1,0:T(2,128)}, u32[]{:S(2)}) copy-start(f32[1,1,2,1024]{3,2,1,0:T(2,128)} %param.12) | copy-start | bytes 24580
  22.5 45.2 %collective-permute-start.6 = (bf16[512,1024]{1,0:T(8,128)(2,1)}, bf16[512,1024]{1,0:T(8,128)(2,1)S(1)}, u32[]{:S(2)}, u32[]{:S(2)}) collective-permute-start(bf16[512,1024]{1,0:T(8,128)(2,1)} %bitcast.1.x_ref), channel_id=1, source_target_pairs={{4,0},{8,4},{12,8},{16,12},{20,16},{24,20},{28,24},{5,1},{9,5},{13... | collective-permute-start | bytes 3145736 | tf_op jit(solution)/shard_map/ppermute | solution.py:339
  39.7 1.0 copy-start.2
  39.7 18.9 %slice-start = ((s8[8388608]{0:T(1024)(128)(4,1)}), s8[4194304]{0:T(1024)(128)(4,1)S(1)}, s32[]{:S(2)}) async-start(s8[8388608]{0:T(1024)(128)(4,1)} %bitcast.31), calls=%async_computation | async-start | bytes 8388608
  39.7 18.9 %slice-start.2 = ((s8[8388608]{0:T(1024)(128)(4,1)}), s8[4194304]{0:T(1024)(128)(4,1)S(1)}, s32[]{:S(2)}) async-start(s8[8388608]{0:T(1024)(128)(4,1)} %bitcast.36), calls=%async_computation.2 | async-start | bytes 8388608
  40.6 17.0 %collective-permute-start.5 = (bf16[256,1152]{1,0:T(8,128)(2,1)S(1)}, bf16[256,1152]{1,0:T(8,128)(2,1)S(1)}, u32[]{:S(2)}, u32[]{:S(2)}) collective-permute-start(bf16[256,1152]{1,0:T(8,128)(2,1)S(1)} %message_part.2), channel_id=1, source_target_pairs={{0,1},{1,2},{2,3},{3,0},{4,5},{5,6},{6,7},{7,4},{8,9},{9,10},{10,1... | collective-permute-start | bytes 1769480 | tf_op jit(solution)/shard_map/ppermute | solution.py:335
  41.2 2.0 %copy-start.3 = (bf16[512,1024]{1,0:T(8,128)(2,1)S(1)}, bf16[512,1024]{1,0:T(8,128)(2,1)}, u32[]{:S(2)}) copy-start(bf16[512,1024]{1,0:T(8,128)(2,1)} %copy-done.2) | copy-start | bytes 3145732
  43.2 0.7 copy-start.8
  43.2 15.4 %slice-start.1 = ((s8[8388608]{0:T(1024)(128)(4,1)}), s8[4194304]{0:T(1024)(128)(4,1)S(1)}, s32[]{:S(2)}) async-start(s8[8388608]{0:T(1024)(128)(4,1)} %bitcast.31), calls=%async_computation.1 | async-start | bytes 8388608
  43.2 15.4 %slice-start.3 = ((s8[8388608]{0:T(1024)(128)(4,1)}), s8[4194304]{0:T(1024)(128)(4,1)S(1)}, s32[]{:S(2)}) async-start(s8[8388608]{0:T(1024)(128)(4,1)} %bitcast.36), calls=%async_computation.3 | async-start | bytes 8388608
  43.9 3.7 %collective-permute-start.1 = (f32[1,1024]{1,0:T(1,128)S(1)}, f32[1,1024]{1,0:T(1,128)S(1)}, u32[]{:S(2)}, u32[]{:S(2)}) collective-permute-start(f32[1,1024]{1,0:T(1,128)S(1)} %copy-done.8), channel_id=1, source_target_pairs={{0,8},{4,12},{8,0},{12,4},{16,24},{20,28},{24,16},{28,20},{1,9},{5... | collective-permute-start | bytes 12296 | tf_op jit(solution)/shard_map/ppermute | solution.py:343
  45.5 3.0 %collective-permute-start.2 = (f32[1,1024]{1,0:T(1,128)S(1)}, f32[1,1024]{1,0:T(1,128)S(1)}, u32[]{:S(2)}, u32[]{:S(2)}) collective-permute-start(f32[1,1024]{1,0:T(1,128)S(1)} %copy-done.8), channel_id=1, source_target_pairs={{0,12},{4,8},{8,4},{12,0},{16,28},{20,24},{24,20},{28,16},{1,13},{... | collective-permute-start | bytes 12296 | tf_op jit(solution)/shard_map/ppermute | solution.py:343
  45.5 3.0 %collective-permute-start.3 = (f32[1,1024]{1,0:T(1,128)S(1)}, f32[1,1024]{1,0:T(1,128)S(1)}, u32[]{:S(2)}, u32[]{:S(2)}) collective-permute-start(f32[1,1024]{1,0:T(1,128)S(1)} %copy-done.8), channel_id=1, source_target_pairs={{0,4},{4,0},{8,12},{12,8},{16,20},{20,16},{24,28},{28,24},{1,5},{5... | collective-permute-start | bytes 12296 | tf_op jit(solution)/shard_map/ppermute | solution.py:343
  67.9 1.6 collective-permute-start.7
  69.6 10.5 %collective-permute-start.8 = (bf16[128,1024]{1,0:T(8,128)(2,1)S(1)}, bf16[128,1024]{1,0:T(8,128)(2,1)S(1)}, u32[]{:S(2)}, u32[]{:S(2)}) collective-permute-start(bf16[128,1024]{1,0:T(8,128)(2,1)S(1)} %get-tuple-element.68), channel_id=1, source_target_pairs={{0,8},{4,12},{8,0},{12,4},{16,24},{20,28},{24,16},{28,20},{1,9},{5... | collective-permute-start | bytes 786440 | tf_op jit(solution)/shard_map/ppermute | solution.py:343
  80.5 1.7 %collective-permute-start.10 = (bf16[128,1024]{1,0:T(8,128)(2,1)S(1)}, bf16[128,1024]{1,0:T(8,128)(2,1)S(1)}, u32[]{:S(2)}, u32[]{:S(2)}) collective-permute-start(bf16[128,1024]{1,0:T(8,128)(2,1)S(1)} %select_convert_fusion.2), channel_id=1, source_target_pairs={{0,4},{4,0},{8,12},{12,8},{16,20},{20,16},{24,28},{28,24},{1,5},{5... | collective-permute-start | bytes 786440 | tf_op jit(solution)/shard_map/ppermute | solution.py:343
  80.6 8.7 %collective-permute-start.9 = (bf16[128,1024]{1,0:T(8,128)(2,1)S(1)}, bf16[128,1024]{1,0:T(8,128)(2,1)S(1)}, u32[]{:S(2)}, u32[]{:S(2)}) collective-permute-start(bf16[128,1024]{1,0:T(8,128)(2,1)S(1)} %fusion.5), channel_id=1, source_target_pairs={{0,16},{4,20},{8,24},{12,28},{16,0},{20,4},{24,8},{28,12},{1,17},{... | collective-permute-start | bytes 786440 | tf_op jit(solution)/shard_map/ppermute | solution.py:343
  82.3 8.4 %collective-permute-start.12 = (bf16[128,1024]{1,0:T(8,128)(2,1)S(1)}, bf16[128,1024]{1,0:T(8,128)(2,1)S(1)}, u32[]{:S(2)}, u32[]{:S(2)}) collective-permute-start(bf16[128,1024]{1,0:T(8,128)(2,1)S(1)} %get-tuple-element.65), channel_id=1, source_target_pairs={{0,8},{4,12},{8,0},{12,4},{16,24},{20,28},{24,16},{28,20},{1,9},{5... | collective-permute-start | bytes 786440 | tf_op jit(solution)/shard_map/ppermute | solution.py:343
  89.5 1.6 collective-permute-start.11
  92.6 8.4 %collective-permute-start.13 = (bf16[128,1024]{1,0:T(8,128)(2,1)S(1)}, bf16[128,1024]{1,0:T(8,128)(2,1)S(1)}, u32[]{:S(2)}, u32[]{:S(2)}) collective-permute-start(bf16[128,1024]{1,0:T(8,128)(2,1)S(1)} %fusion.8), channel_id=1, source_target_pairs={{0,16},{4,20},{8,24},{12,28},{16,0},{20,4},{24,8},{28,12},{1,17},{... | collective-permute-start | bytes 786440 | tf_op jit(solution)/shard_map/ppermute | solution.py:343
  94.2 16.7 %collective-permute-start.15 = (bf16[256,1024]{1,0:T(8,128)(2,1)S(1)}, bf16[256,1024]{1,0:T(8,128)(2,1)S(1)}, u32[]{:S(2)}, u32[]{:S(2)}) collective-permute-start(bf16[256,1024]{1,0:T(8,128)(2,1)S(1)} %fusion), channel_id=1, source_target_pairs={{0,1},{1,2},{2,3},{3,0},{4,5},{5,6},{6,7},{7,4},{8,9},{9,10},{10,1... | collective-permute-start | bytes 1572872 | tf_op jit(solution)/shard_map/ppermute | solution.py:335
  101.2 1.6 collective-permute-start.14
  101.3 21.0 %collective-permute-start.16 = (bf16[256,1024]{1,0:T(8,128)(2,1)S(1)}, bf16[256,1024]{1,0:T(8,128)(2,1)S(1)}, u32[]{:S(2)}, u32[]{:S(2)}) collective-permute-start(bf16[256,1024]{1,0:T(8,128)(2,1)S(1)} %fusion), channel_id=1, source_target_pairs={{1,0},{2,1},{3,2},{5,4},{6,5},{7,6},{9,8},{10,9},{11,10},{13,12},{... | collective-permute-start | bytes 1572872 | tf_op jit(solution)/shard_map/ppermute | solution.py:339
  111.1 1.4 copy-start.5
  112.3 19.9 %collective-permute-start.17 = (bf16[256,1024]{1,0:T(8,128)(2,1)S(1)}, bf16[256,1024]{1,0:T(8,128)(2,1)S(1)}, u32[]{:S(2)}, u32[]{:S(2)}) collective-permute-start(bf16[256,1024]{1,0:T(8,128)(2,1)S(1)} %fusion.1), channel_id=1, source_target_pairs={{0,1},{1,2},{2,3},{3,0},{4,5},{5,6},{6,7},{7,4},{8,9},{9,10},{10,1... | collective-permute-start | bytes 1572872 | tf_op jit(solution)/shard_map/ppermute | solution.py:335
  133.2 16.0 %collective-permute-start.18 = (bf16[256,1152]{1,0:T(8,128)(2,1)S(1)}, bf16[256,1152]{1,0:T(8,128)(2,1)S(1)}, u32[]{:S(2)}, u32[]{:S(2)}) collective-permute-start(bf16[256,1152]{1,0:T(8,128)(2,1)S(1)} %message_part.3), channel_id=1, source_target_pairs={{0,1},{1,2},{2,3},{3,0},{4,5},{5,6},{6,7},{7,4},{8,9},{9,10},{10,1... | collective-permute-start | bytes 1769480 | tf_op jit(solution)/shard_map/ppermute | solution.py:335

commit v2 on v1

--- a/solution.py
+++ b/solution.py
@@ -210,12 +210,8 @@
         )
 
 
-def finish_kernel(
-    first, x_ref, num_ref, den_ref, w_ref, gain_ref, up_ref, down_ref, out_ref, acc_ref, n_ref, hidden_ref
-):
-    rows, width = out_ref.shape
-    hidden = up_ref.shape[1]
-    tile = min(TILE, hidden)
+def mix(first, x_ref, num_ref, den_ref, w_ref, gain_ref, acc_ref, n_ref):
+    rows, width = acc_ref.shape
     here = pl.ds(first, rows)
     lane = lax.broadcasted_iota(jnp.int32, (rows, LANES), 1)
     inverse = 1.0 / jnp.where(lane < HEADS, den_ref[here], 1.0)
@@ -223,23 +219,50 @@
     acc_ref[...] = x_ref[here].astype(F32) + dot(n_ref[...], w_ref[3])
     n_ref[...] = rms_norm(acc_ref[...], gain_ref[1:2]).astype(BF16)
 
+
+def feed_forward(begin, end, n_ref, up_ref, down_ref, acc_ref, hidden_ref):
+    tile = hidden_ref.shape[2]
+
     def expand(j):
         cols = pl.ds(pl.multiple_of(j * tile, tile), tile)
         return jax.nn.gelu(dot(n_ref[...], up_ref[:, cols])).astype(BF16)
 
-    def lower(j, expanded):
-        return dot(expanded, down_ref[pl.ds(pl.multiple_of(j * tile, tile), tile)])
-
-    hidden_ref[0] = expand(0)
+    def lower(j):
+        return dot(hidden_ref[j % 2], down_ref[pl.ds(pl.multiple_of(j * tile, tile), tile)])
+
+    hidden_ref[begin % 2] = expand(begin)
 
     def one(j, carry):
-        acc_ref[...] += lower(j, hidden_ref[j % 2])
+        acc_ref[...] += lower(j)
         hidden_ref[(j + 1) % 2] = expand(j + 1)
         return carry
 
-    last = hidden // tile - 1
-    lax.fori_loop(0, last, one, 0)
-    out_ref[...] = (acc_ref[...] + lower(last, hidden_ref[last % 2])).astype(BF16)
+    lax.fori_loop(begin, end - 1, one, 0)
+    return lower(end - 1)
+
+
+def finish_kernel(
+    first, x_ref, num_ref, den_ref, w_ref, gain_ref, up_ref, down_ref, out_ref, acc_ref, n_ref, hidden_ref
+):
+    mix(first, x_ref, num_ref, den_ref, w_ref, gain_ref, acc_ref, n_ref)
+    tiles = up_ref.shape[1] // hidden_ref.shape[2]
+    last = feed_forward(0, tiles, n_ref, up_ref, down_ref, acc_ref, hidden_ref)
+    out_ref[...] = (acc_ref[...] + last).astype(BF16)
+
+
+def open_kernel(
+    first, tiles, x_ref, num_ref, den_ref, w_ref, gain_ref, up_ref, down_ref, acc_ref, n_ref, hidden_ref
+):
+    mix(first, x_ref, num_ref, den_ref, w_ref, gain_ref, acc_ref, n_ref)
+    last = feed_forward(0, tiles, n_ref, up_ref, down_ref, acc_ref, hidden_ref)
+    acc_ref[...] += last
+
+
+def close_kernel(begin, acc_in, n_ref, up_ref, down_ref, out_ref, acc_ref, hidden_ref):
+    acc_ref[...] = acc_in[...]
+    tiles = up_ref.shape[1] // hidden_ref.shape[2]
+    last = feed_forward(begin, tiles, n_ref, up_ref, down_ref, acc_ref, hidden_ref)
+    out_ref[...] = (acc_ref[...] + last).astype(BF16)
 
 
 def vmem():
@@ -330,13 +353,34 @@
     )[0]
 
 
+def open_part(x, num, den, weights, gains, part, parts, tiles):
+    width = x.shape[1]
+    rows = x.shape[0] // parts
+    return call(
+        functools.partial(open_kernel, part * rows, tiles),
+        "open_part",
+        (x, num, den, weights[0], gains, *weights[1:]),
+        None,
+        [((rows, width), F32), ((rows, width), BF16)],
+        [pltpu.VMEM((2, rows, min(TILE, weights[1].shape[1])), BF16)],
+    )
+
+
+def close_part(acc, n, weights, tiles):
+    return call(
+        functools.partial(close_kernel, tiles),
+        "close_part",
+        (acc, n, *weights[1:]),
+        None,
+        [(acc.shape, BF16)],
+        [pltpu.VMEM(acc.shape, F32), pltpu.VMEM((2, acc.shape[0], min(TILE, weights[1].shape[1])), BF16)],
+    )[0]
+
+
 def shifted(value, axis, steps):
     count = lax.axis_size(axis)
-    return lax.ppermute(value, axis, [(i, (i + steps) % count) for i in range(count)])
-
-
-def sent_back(value, axis):
-    return lax.ppermute(value, axis, [(i, i - 1) for i in range(1, lax.axis_size(axis))])
+    first, last = max(0, -steps), min(count, count - steps)
+    return lax.ppermute(value, axis, [(i, i + steps) for i in range(first, last)])
 
 
 def swapped(value, axis, bit):
@@ -447,7 +491,7 @@
     weights = (w_attn[0, 0], w_up[0, 0], w_down[0, 0])
     parts = [x[:half], x[half:]]
     piece = shifted(x, "seq", 1)
-    first_back = sent_back(parts[0], "seq")
+    first_back = shifted(parts[0], "seq", -1)
     docs = Documents(doc_ids, rows)
     place, bits, bit = lax.axis_index("depth"), {}, 1
     while bit < lax.axis_size("depth"):
@@ -457,23 +501,27 @@
         (x, bits, docs.own_column, docs.later_column)
     )
     state = own_part(early, gains, weights, docs)
-    following = sent_back(after(x, state[0]), "depth")
+    following = shifted(after(x, state[0]), "depth", -1)
     (num, den), factors = attention(
         state, piece, first_back, docs, gains, weights[0], lambda token: gain_factors(after(coarse_gain, token), bits)
     )
     following = [following[:half], following[half:]]
     first, second = [Chain(parts[i], following[i], factors, bits) for i in range(2)]
     first.enter(finish_part(x, num, den, weights, gains, 0, 2))
-    fine = finish_part(x, after(num, first.total), den, weights, gains, 1, 2)
-    first.level(0)
-    second.enter(fine, first.total)
-    for i in range(1, len(first.levels)):
-        second.level(i - 1)
-        first.level(i, used_after=(second.entered,))
+    tiles = weights[1].shape[1] // TILE // 2
+    acc, n = open_part(x, after(num, first.total), den, weights, gains, 1, 2, tiles)
+    first.level(0, used_after=(n,))
+    fine = close_part(after(acc, first.total), n, weights, tiles)
+    first.level(1, used_after=(fine,))
+    second.enter(fine, first.before)
+    for i in range(2, len(first.levels)):
+        second.level(i - 2)
+        first.level(i)
     corrected = [first.leave()]
     halves = [shifted(corrected[0], "seq", 1)]
-    first_back = sent_back(corrected[0], "seq")
-    second.level(len(first.levels) - 1, sent_after=(corrected[0],))
+    first_back = shifted(corrected[0], "seq", -1)
+    for i in range(max(0, len(first.levels) - 2), len(first.levels)):
+        second.level(i, sent_after=(corrected[0],) if i > 0 else ())
     corrected.append(second.leave(used_after=(halves[0],)))
     halves.append(shifted(corrected[1], "seq", 1))
     x = jnp.concatenate(corrected, axis=0)

time: 166 us -> 146 us (0.88)
  the two profiles are of different devices: /device:TPU:0 before, /device:TPU:8 now
where the time goes in v2:
time: 146 us; the launch traced here: 145 us
  Pallas kernels  72.2 us (49%)
  waiting for transfers between devices  32.6 us (22%)
  starting transfers between devices  26.2 us (18%)
  local copies, waits for them, and re-layouts  11.1 us (8%)
  other arithmetic  2.27 us (2%)
    pallas_call x12, Pallas kernels, call(): pl.pallas_call(kernel, in_specs=in_specs, out_specs=[vmem()] * len(result...  72.2 us
    ppermute x11, waiting for transfers between devices, swapped(): lax.ppermute(value, axis, [(i, i ^ bit) for i in range(lax.axis_size(axis...  20.7 us
    ppermute x8, starting transfers between devices, shifted(): lax.ppermute(value, axis, [(i, i + steps) for i in range(first, last)])  19.7 us
    ppermute x8, waiting for transfers between devices, shifted(): lax.ppermute(value, axis, [(i, i + steps) for i in range(first, last)])  11.9 us
    unnamed x29, local copies, waits for them, and re-layouts  8.24 us
    ppermute x11, starting transfers between devices, swapped(): lax.ppermute(value, axis, [(i, i ^ bit) for i in range(lax.axis_size(axis...  6.47 us
  transfers between devices with their start and end apart: 19, of which 11 were waited for; matrix products, arithmetic and copies ran while one was open for 3% of the time, Pallas kernels for 39%

profile of v2, /device:TPU:8, one launch (start us, length us, event | category | flops | bytes accessed | tf_op | source)
XLA Modules:
  0.0 144.9 jit_solution(12260793409388769759)
XLA Ops:
  0.0 3.6 %collective-permute-start = (bf16[512,1024]{1,0:T(8,128)(2,1)}, bf16[512,1024]{1,0:T(8,128)(2,1)S(1)}, u32[]{:S(2)}, u32[]{:S(2)}) collective-permute-start(bf16[512,1024]{1,0:T(8,128)(2,1)} %bitcast.45), channel_id=1, source_target_pairs={{0,1},{1,2},{2,3},{4,5},{5,6},{6,7},{8,9},{9,10},{10,11},{12,13},{... | collective-permute-start | bytes 3145736 | tf_op jit(solution)/shard_map/ppermute | solution.py:383
  3.6 1.1 slice_bitcast_fusion
  4.7 2.4 %collective-permute-start.4 = (bf16[256,1024]{1,0:T(8,128)(2,1)S(1)}, bf16[256,1024]{1,0:T(8,128)(2,1)S(1)}, u32[]{:S(2)}, u32[]{:S(2)}) collective-permute-start(bf16[256,1024]{1,0:T(8,128)(2,1)S(1)} %slice_bitcast_fusion), channel_id=1, source_target_pairs={{1,0},{2,1},{3,2},{5,4},{6,5},{7,6},{9,8},{10,9},{11,10},{13,12},{... | collective-permute-start | bytes 1572872 | tf_op jit(solution)/shard_map/ppermute | solution.py:383
  7.1 0.8 constant_dynamic-slice_fusion.1
  7.9 0.8 constant_dynamic-slice_fusion
  8.7 0.1 broadcast_in_dim.21.column_ref
  8.8 0.1 broadcast_in_dim.23.column_ref
  8.9 3.4 %copy-done = bf16[1,1,4,1024,1024]{4,3,2,1,0:T(8,128)(2,1)S(1)} copy-done((bf16[1,1,4,1024,1024]{4,3,2,1,0:T(8,128)(2,1)S(1)}, bf16[1,1,4,1024,1024]{4,3,2,1,0:T(8,128)(2,1)}, u32[]{:S(2)}) %copy-start) | copy-done | bytes 8388632
  12.3 0.7 copy-done.4
  13.0 0.7 copy-done.5
  13.7 9.8 %own_part.2 = (bf16[3,512,1024]{2,1,0:T(8,128)(2,1)S(1)}, f32[512,1024]{1,0:T(8,128)S(1)}, f32[512,128]{1,0:T(8,128)S(1)}) custom-call(bf16[512,1024]{1,0:T(8,128)(2,1)S(1)} %bitcast.46, f32[2,1024]{1,0:T(2,128)S(1)} %bitcast.50, bf16[4,1024,1024]{2,1,0:T(8,128)(2,1)S(1)} %bitcast.20, s32[512,128]{1,0:T(8,128)S(1)} %broadcast_in_dim.21.column_ref, ...), custom_call_target="tpu_custom_call" | custom-call | flops 1048576 | bytes 65536 | tf_op jit(solution)/shard_map/own_part/pallas_call | solution.py:278
  23.5 1.3 collective-permute-start.6
  24.8 2.3 %collective-permute-done.x_ref.piece_ref = bf16[512,1024]{1,0:T(8,128)(2,1)S(1)} collective-permute-done((bf16[512,1024]{1,0:T(8,128)(2,1)}, bf16[512,1024]{1,0:T(8,128)(2,1)S(1)}, u32[]{:S(2)}, u32[]{:S(2)}) %collective-permute-start) | collective-permute-done | bytes 1048608 | tf_op jit(solution)/shard_map/ppermute | solution.py:383
  27.1 0.7 message_part.2
  27.9 3.7 %collective-permute-start.5 = (bf16[256,1152]{1,0:T(8,128)(2,1)S(1)}, bf16[256,1152]{1,0:T(8,128)(2,1)S(1)}, u32[]{:S(2)}, u32[]{:S(2)}) collective-permute-start(bf16[256,1152]{1,0:T(8,128)(2,1)S(1)} %message_part.2), channel_id=1, source_target_pairs={{0,1},{1,2},{2,3},{4,5},{5,6},{6,7},{8,9},{9,10},{10,11},{12,13},{... | collective-permute-start | bytes 1769480 | tf_op jit(solution)/shard_map/ppermute | solution.py:383
  31.7 9.6 %piece_part.2 = (f32[512,1024]{1,0:T(8,128)S(1)}, f32[512,128]{1,0:T(8,128)S(1)}) custom-call(bf16[512,1024]{1,0:T(8,128)(2,1)S(1)} %collective-permute-done.x_ref.piece_ref, f32[2,1024]{1,0:T(2,128)S(1)} %bitcast.52, bf16[4,1024,1024]{2,1,0:T(8,128)(2,1)S(1)} %bitcast.22, ...), custom_call_target="tpu_custom_call", output_to_operand_aliasing={{0}: (4, {}), {1}: (5, {})} | custom-call | flops 1048576 | bytes 65536 | tf_op jit(solution)/shard_map/piece_part/pallas_call | solution.py:278
  41.3 1.6 %collective-permute-start.1 = (f32[1,1024]{1,0:T(1,128)S(1)}, f32[1,1024]{1,0:T(1,128)S(1)}, u32[]{:S(2)}, u32[]{:S(2)}) collective-permute-start(f32[1,1024]{1,0:T(1,128)S(1)} %copy-done.7), channel_id=1, source_target_pairs={{0,8},{4,12},{8,0},{12,4},{16,24},{20,28},{24,16},{28,20},{1,9},{5... | collective-permute-start | bytes 12296 | tf_op jit(solution)/shard_map/ppermute | solution.py:387
  42.8 0.6 collective-permute-start.3
  43.5 1.5 %collective-permute-done.1 = f32[1,1024]{1,0:T(1,128)S(1)} collective-permute-done((f32[1,1024]{1,0:T(1,128)S(1)}, f32[1,1024]{1,0:T(1,128)S(1)}, u32[]{:S(2)}, u32[]{:S(2)}) %collective-permute-start.1) | collective-permute-done | bytes 4128 | tf_op jit(solution)/shard_map/ppermute | solution.py:387
  44.9 0.9 collective-permute-done.2
  45.9 0.9 reply_part.2
  46.8 7.7 %finish_part.2 = bf16[256,1024]{1,0:T(8,128)(2,1)S(1)} custom-call(bf16[512,1024]{1,0:T(8,128)(2,1)S(1)} %bitcast.48, f32[512,1024]{1,0:T(8,128)S(1)} %get-tuple-element.56.num_ref, f32[512,128]{1,0:T(8,128)S(1)} %get-tuple-element.54.den_ref, bf16[4,1024,1024]{2,1,0:T(8,128)(2,1)S(1)} %bitcast.24, f32[2,1024]{1,0:T(2,128)S(1)} %bitcast.54, ...), custom_call_target="tpu_custom_call" | custom-call | flops 1048576 | bytes 65536 | tf_op jit(solution)/shard_map/finish_part/pallas_call | solution.py:278
  54.6 0.2 convert_subtract_fusion.1
  54.8 0.1 select_convert_fusion.3
  54.8 0.1 collective-permute-start.7
  54.9 1.5 %collective-permute-done.7 = bf16[128,1024]{1,0:T(8,128)(2,1)S(1)} collective-permute-done((bf16[128,1024]{1,0:T(8,128)(2,1)S(1)}, bf16[128,1024]{1,0:T(8,128)(2,1)S(1)}, u32[]{:S(2)}, u32[]{:S(2)}) %collective-permute-start.7) | collective-permute-done | bytes 262176 | tf_op jit(solution)/shard_map/ppermute | solution.py:387
  56.4 0.2 fusion.12
  56.6 0.6 collective-permute-start.8
  57.2 4.5 %open_part.1 = (f32[256,1024]{1,0:T(8,128)S(1)}, bf16[256,1024]{1,0:T(8,128)(2,1)S(1)}) custom-call(bf16[512,1024]{1,0:T(8,128)(2,1)S(1)} %bitcast.49, f32[512,1024]{1,0:T(8,128)S(1)} %get-tuple-element.56.num_ref, f32[512,128]{1,0:T(8,128)S(1)} %get-tuple-element.54.den_ref, bf16[4,1024,1024]{2,1,0:T(8,128)(2,1)S(1)} %bitcast.25, f32[2,1024]{1,0:T(2,128)S(1)} %bitcast.55, ...), custom_call_target="tpu_custom_call" | custom-call | flops 1048576 | bytes 65536 | tf_op jit(solution)/shard_map/open_part/pallas_call | solution.py:278
  61.7 3.3 %collective-permute-done.8 = bf16[128,1024]{1,0:T(8,128)(2,1)S(1)} collective-permute-done((bf16[128,1024]{1,0:T(8,128)(2,1)S(1)}, bf16[128,1024]{1,0:T(8,128)(2,1)S(1)}, u32[]{:S(2)}, u32[]{:S(2)}) %collective-permute-start.8) | collective-permute-done | bytes 262176 | tf_op jit(solution)/shard_map/ppermute | solution.py:387
  65.0 0.1 fusion.5
  65.1 1.6 %collective-permute-start.9 = (bf16[128,1024]{1,0:T(8,128)(2,1)S(1)}, bf16[128,1024]{1,0:T(8,128)(2,1)S(1)}, u32[]{:S(2)}, u32[]{:S(2)}) collective-permute-start(bf16[128,1024]{1,0:T(8,128)(2,1)S(1)} %fusion.5), channel_id=1, source_target_pairs={{0,16},{4,20},{8,24},{12,28},{16,0},{20,4},{24,8},{28,12},{1,17},{... | collective-permute-start | bytes 786440 | tf_op jit(solution)/shard_map/ppermute | solution.py:387
  66.7 3.4 %copy-done.2 = bf16[1,1,4096,1024]{3,2,1,0:T(8,128)(2,1)S(1)} copy-done((bf16[1,1,4096,1024]{3,2,1,0:T(8,128)(2,1)S(1)}, bf16[1,1,4096,1024]{3,2,1,0:T(8,128)(2,1)}, u32[]{:S(2)}) %copy-start.2) | copy-done | bytes 8388632
  70.1 3.5 %close_part.1 = bf16[256,1024]{1,0:T(8,128)(2,1)S(1)} custom-call(f32[256,1024]{1,0:T(8,128)S(1)} %get-tuple-element.60.acc_in, bf16[256,1024]{1,0:T(8,128)(2,1)S(1)} %get-tuple-element.57.n_ref, bf16[1024,4096]{1,0:T(8,128)(2,1)S(1)} %bitcast.35, bf16[4096,1024]{1,0:T(8,128)(2,1)S(1)} %bitcast.41), custom_call_target="tpu_custom_call" | custom-call | flops 1048576 | bytes 65536 | tf_op jit(solution)/shard_map/close_part/pallas_call | solution.py:278
  73.6 0.2 select_convert_fusion.2
  73.8 0.2 convert_subtract_fusion
  74.1 0.1 collective-permute-start.11
  74.2 0.5 collective-permute-start.10
  74.7 1.0 collective-permute-done.11
  75.7 0.1 fusion.11
  75.8 0.6 collective-permute-start.12
  76.5 0.2 convert_select_fusion.7
  76.7 0.1 fusion
  76.8 7.4 %collective-permute-done.12 = bf16[128,1024]{1,0:T(8,128)(2,1)S(1)} collective-permute-done((bf16[128,1024]{1,0:T(8,128)(2,1)S(1)}, bf16[128,1024]{1,0:T(8,128)(2,1)S(1)}, u32[]{:S(2)}, u32[]{:S(2)}) %collective-permute-start.12) | collective-permute-done | bytes 262176 | tf_op jit(solution)/shard_map/ppermute | solution.py:387
  84.2 0.2 fusion.8
  84.4 0.7 collective-permute-start.13
  85.1 1.9 %collective-permute-start.15 = (bf16[256,1024]{1,0:T(8,128)(2,1)S(1)}, bf16[256,1024]{1,0:T(8,128)(2,1)S(1)}, u32[]{:S(2)}, u32[]{:S(2)}) collective-permute-start(bf16[256,1024]{1,0:T(8,128)(2,1)S(1)} %fusion), channel_id=1, source_target_pairs={{0,1},{1,2},{2,3},{4,5},{5,6},{6,7},{8,9},{9,10},{10,11},{12,13},{... | collective-permute-start | bytes 1572872 | tf_op jit(solution)/shard_map/ppermute | solution.py:383
  87.0 5.0 %collective-permute-done.13 = bf16[128,1024]{1,0:T(8,128)(2,1)S(1)} collective-permute-done((bf16[128,1024]{1,0:T(8,128)(2,1)S(1)}, bf16[128,1024]{1,0:T(8,128)(2,1)S(1)}, u32[]{:S(2)}, u32[]{:S(2)}) %collective-permute-start.13) | collective-permute-done | bytes 262176 | tf_op jit(solution)/shard_map/ppermute | solution.py:387
  92.0 0.2 select_convert_fusion
  92.2 0.1 collective-permute-start.14
  92.3 1.9 %collective-permute-start.16 = (bf16[256,1024]{1,0:T(8,128)(2,1)S(1)}, bf16[256,1024]{1,0:T(8,128)(2,1)S(1)}, u32[]{:S(2)}, u32[]{:S(2)}) collective-permute-start(bf16[256,1024]{1,0:T(8,128)(2,1)S(1)} %fusion), channel_id=1, source_target_pairs={{1,0},{2,1},{3,2},{5,4},{6,5},{7,6},{9,8},{10,9},{11,10},{13,12},{... | collective-permute-start | bytes 1572872 | tf_op jit(solution)/shard_map/ppermute | solution.py:383
  94.3 5.6 %collective-permute-done.15 = bf16[256,1024]{1,0:T(8,128)(2,1)S(1)} collective-permute-done((bf16[256,1024]{1,0:T(8,128)(2,1)S(1)}, bf16[256,1024]{1,0:T(8,128)(2,1)S(1)}, u32[]{:S(2)}, u32[]{:S(2)}) %collective-permute-start.15) | collective-permute-done | bytes 524320 | tf_op jit(solution)/shard_map/ppermute | solution.py:383
  99.9 0.3 convert_select_fusion.3
  100.1 0.1 fusion.1
  100.3 2.2 %collective-permute-start.17 = (bf16[256,1024]{1,0:T(8,128)(2,1)S(1)}, bf16[256,1024]{1,0:T(8,128)(2,1)S(1)}, u32[]{:S(2)}, u32[]{:S(2)}) collective-permute-start(bf16[256,1024]{1,0:T(8,128)(2,1)S(1)} %fusion.1), channel_id=1, source_target_pairs={{0,1},{1,2},{2,3},{4,5},{5,6},{6,7},{8,9},{9,10},{10,11},{12,13},{... | collective-permute-start | bytes 1572872 | tf_op jit(solution)/shard_map/ppermute | solution.py:383
  102.5 0.1 pad_maximum_fusion.x_ref
  102.6 9.7 %own_part.3 = (bf16[3,512,1024]{2,1,0:T(8,128)(2,1)S(1)}, f32[512,1024]{1,0:T(8,128)S(1)}, f32[512,128]{1,0:T(8,128)S(1)}) custom-call(bf16[512,1024]{1,0:T(8,128)(2,1)S(1)} %pad_maximum_fusion.x_ref, f32[2,1024]{1,0:T(2,128)S(1)} %bitcast.56, bf16[4,1024,1024]{2,1,0:T(8,128)(2,1)S(1)} %bitcast.26, s32[512,128]{1,0:T(8,128)S(1)} %broadcast_in_dim.21.column_ref, ...), custom_call_target="tpu_custom_call" | custom-call | flops 1048576 | bytes 65536 | tf_op jit(solution)/shard_map/own_part/pallas_call | solution.py:278
  112.4 1.7 %collective-permute-done.17 = bf16[256,1024]{1,0:T(8,128)(2,1)S(1)} collective-permute-done((bf16[256,1024]{1,0:T(8,128)(2,1)S(1)}, bf16[256,1024]{1,0:T(8,128)(2,1)S(1)}, u32[]{:S(2)}, u32[]{:S(2)}) %collective-permute-start.17) | collective-permute-done | bytes 524320 | tf_op jit(solution)/shard_map/ppermute | solution.py:383
  114.2 0.9 message_part.3
  115.1 2.6 %collective-permute-start.18 = (bf16[256,1152]{1,0:T(8,128)(2,1)S(1)}, bf16[256,1152]{1,0:T(8,128)(2,1)S(1)}, u32[]{:S(2)}, u32[]{:S(2)}) collective-permute-start(bf16[256,1152]{1,0:T(8,128)(2,1)S(1)} %message_part.3), channel_id=1, source_target_pairs={{0,1},{1,2},{2,3},{4,5},{5,6},{6,7},{8,9},{9,10},{10,11},{12,13},{... | collective-permute-start | bytes 1769480 | tf_op jit(solution)/shard_map/ppermute | solution.py:383
  117.7 9.5 %piece_part.3 = (f32[512,1024]{1,0:T(8,128)S(1)}, f32[512,128]{1,0:T(8,128)S(1)}) custom-call(bf16[512,1024]{1,0:T(8,128)(2,1)S(1)} %constant_dynamic-update-slice_fusion.piece_ref.x_ref, f32[2,1024]{1,0:T(2,128)S(1)} %bitcast.58, bf16[4,1024,1024]{2,1,0:T(8,128)(2,1)S(1)} %bitcast.28, ...), custom_call_target="tpu_custom_call", output_to_operand_aliasing={{0}: (4, {}), {1}: (5, {})} | custom-call | flops 1048576 | bytes 65536 | tf_op jit(solution)/shard_map/piece_part/pallas_call | solution.py:278
  127.3 2.3 %collective-permute-done.18.message_ref = bf16[256,1152]{1,0:T(8,128)(2,1)S(1)} collective-permute-done((bf16[256,1152]{1,0:T(8,128)(2,1)S(1)}, bf16[256,1152]{1,0:T(8,128)(2,1)S(1)}, u32[]{:S(2)}, u32[]{:S(2)}) %collective-permute-start.18) | collective-permute-done | bytes 589856 | tf_op jit(solution)/shard_map/ppermute | solution.py:383
  129.5 0.7 reply_part.3
  130.3 14.6 %finish_part.3 = bf16[512,1024]{1,0:T(8,128)(2,1)} custom-call(bf16[512,1024]{1,0:T(8,128)(2,1)S(1)} %pad_maximum_fusion.x_ref, f32[512,1024]{1,0:T(8,128)S(1)} %get-tuple-element.71.num_ref, f32[512,128]{1,0:T(8,128)S(1)} %get-tuple-element.72.den_ref, bf16[4,1024,1024]{2,1,0:T(8,128)(2,1)S(1)} %bitcast.30, f32[2,1024]{1,0:T(2,128)S(1)} %bitcast.60, ...), custom_call_target="tpu_custom_call" | custom-call | flops 1048576 | bytes 65536 | tf_op jit(solution)/shard_map/finish_part/pallas_call | solution.py:278
  (41 shorter events, 0.2 us)
Async XLA Ops:
  0.0 8.9 %copy-start.3 = (bf16[1,1,512,1024]{3,2,1,0:T(8,128)(2,1)S(1)}, bf16[1,1,512,1024]{3,2,1,0:T(8,128)(2,1)}, u32[]{:S(2)}) copy-start(bf16[1,1,512,1024]{3,2,1,0:T(8,128)(2,1)} %param.7) | copy-start | bytes 3145732
  0.0 27.1 %collective-permute-start = (bf16[512,1024]{1,0:T(8,128)(2,1)}, bf16[512,1024]{1,0:T(8,128)(2,1)S(1)}, u32[]{:S(2)}, u32[]{:S(2)}) collective-permute-start(bf16[512,1024]{1,0:T(8,128)(2,1)} %bitcast.45), channel_id=1, source_target_pairs={{0,1},{1,2},{2,3},{4,5},{5,6},{6,7},{8,9},{9,10},{10,11},{12,13},{... | collective-permute-start | bytes 3145736 | tf_op jit(solution)/shard_map/ppermute | solution.py:383
  4.7 20.1 %collective-permute-start.4 = (bf16[256,1024]{1,0:T(8,128)(2,1)S(1)}, bf16[256,1024]{1,0:T(8,128)(2,1)S(1)}, u32[]{:S(2)}, u32[]{:S(2)}) collective-permute-start(bf16[256,1024]{1,0:T(8,128)(2,1)S(1)} %slice_bitcast_fusion), channel_id=1, source_target_pairs={{1,0},{2,1},{3,2},{5,4},{6,5},{7,6},{9,8},{10,9},{11,10},{13,12},{... | collective-permute-start | bytes 1572872 | tf_op jit(solution)/shard_map/ppermute | solution.py:383
  8.9 3.4 %copy-start = (bf16[1,1,4,1024,1024]{4,3,2,1,0:T(8,128)(2,1)S(1)}, bf16[1,1,4,1024,1024]{4,3,2,1,0:T(8,128)(2,1)}, u32[]{:S(2)}) copy-start(bf16[1,1,4,1024,1024]{4,3,2,1,0:T(8,128)(2,1)} %param.9) | copy-start | bytes 25165828
  12.3 0.7 copy-start.4
  13.0 0.7 copy-start.5
  13.7 13.5 %copy-start.1 = (bf16[1,1,4,1024,1024]{4,3,2,1,0:T(8,128)(2,1)S(1)}, bf16[1,1,4,1024,1024]{4,3,2,1,0:T(8,128)(2,1)}, u32[]{:S(2)}) copy-start(bf16[1,1,4,1024,1024]{4,3,2,1,0:T(8,128)(2,1)} %param.9) | copy-start | bytes 25165828
  13.7 13.5 %copy-start.6 = (f32[1,1,2,1024]{3,2,1,0:T(2,128)S(1)}, f32[1,1,2,1024]{3,2,1,0:T(2,128)}, u32[]{:S(2)}) copy-start(f32[1,1,2,1024]{3,2,1,0:T(2,128)} %param.12) | copy-start | bytes 24580
  23.5 31.1 %collective-permute-start.6 = (bf16[512,1024]{1,0:T(8,128)(2,1)S(1)}, bf16[512,1024]{1,0:T(8,128)(2,1)S(1)}, u32[]{:S(2)}, u32[]{:S(2)}) collective-permute-start(bf16[512,1024]{1,0:T(8,128)(2,1)S(1)} %bitcast.47), channel_id=1, source_target_pairs={{4,0},{8,4},{12,8},{16,12},{20,16},{24,20},{28,24},{5,1},{9,5},{13... | collective-permute-start | bytes 3145736 | tf_op jit(solution)/shard_map/ppermute | solution.py:383
  27.1 19.7 %slice-start = ((s8[8388608]{0:T(1024)(128)(4,1)}), s8[4194304]{0:T(1024)(128)(4,1)S(1)}, s32[]{:S(2)}) async-start(s8[8388608]{0:T(1024)(128)(4,1)} %bitcast.31), calls=%async_computation | async-start | bytes 8388608
  27.1 19.7 %slice-start.2 = ((s8[8388608]{0:T(1024)(128)(4,1)}), s8[4194304]{0:T(1024)(128)(4,1)S(1)}, s32[]{:S(2)}) async-start(s8[8388608]{0:T(1024)(128)(4,1)} %bitcast.37), calls=%async_computation.2 | async-start | bytes 8388608
  27.9 18.0 %collective-permute-start.5 = (bf16[256,1152]{1,0:T(8,128)(2,1)S(1)}, bf16[256,1152]{1,0:T(8,128)(2,1)S(1)}, u32[]{:S(2)}, u32[]{:S(2)}) collective-permute-start(bf16[256,1152]{1,0:T(8,128)(2,1)S(1)} %message_part.2), channel_id=1, source_target_pairs={{0,1},{1,2},{2,3},{4,5},{5,6},{6,7},{8,9},{9,10},{10,11},{12,13},{... | collective-permute-start | bytes 1769480 | tf_op jit(solution)/shard_map/ppermute | solution.py:383
  31.6 9.6 %copy-start.7 = (f32[1,1024]{1,0:T(1,128)S(1)}, f32[1,1024]{1,0:T(1,128)}, u32[]{:S(2)}) copy-start(f32[1,1024]{1,0:T(1,128)} %param.13) | copy-start | bytes 12292
  31.6 15.2 %slice-start.1 = ((s8[8388608]{0:T(1024)(128)(4,1)}), s8[4194304]{0:T(1024)(128)(4,1)S(1)}, s32[]{:S(2)}) async-start(s8[8388608]{0:T(1024)(128)(4,1)} %bitcast.31), calls=%async_computation.1 | async-start | bytes 8388608
  31.6 15.2 %slice-start.3 = ((s8[8388608]{0:T(1024)(128)(4,1)}), s8[4194304]{0:T(1024)(128)(4,1)S(1)}, s32[]{:S(2)}) async-start(s8[8388608]{0:T(1024)(128)(4,1)} %bitcast.37), calls=%async_computation.3 | async-start | bytes 8388608
  41.3 3.7 %collective-permute-start.1 = (f32[1,1024]{1,0:T(1,128)S(1)}, f32[1,1024]{1,0:T(1,128)S(1)}, u32[]{:S(2)}, u32[]{:S(2)}) collective-permute-start(f32[1,1024]{1,0:T(1,128)S(1)} %copy-done.7), channel_id=1, source_target_pairs={{0,8},{4,12},{8,0},{12,4},{16,24},{20,28},{24,16},{28,20},{1,9},{5... | collective-permute-start | bytes 12296 | tf_op jit(solution)/shard_map/ppermute | solution.py:387
  42.8 3.0 %collective-permute-start.2 = (f32[1,1024]{1,0:T(1,128)S(1)}, f32[1,1024]{1,0:T(1,128)S(1)}, u32[]{:S(2)}, u32[]{:S(2)}) collective-permute-start(f32[1,1024]{1,0:T(1,128)S(1)} %copy-done.7), channel_id=1, source_target_pairs={{0,12},{4,8},{8,4},{12,0},{16,28},{20,24},{24,20},{28,16},{1,13},{... | collective-permute-start | bytes 12296 | tf_op jit(solution)/shard_map/ppermute | solution.py:387
  42.8 3.0 %collective-permute-start.3 = (f32[1,1024]{1,0:T(1,128)S(1)}, f32[1,1024]{1,0:T(1,128)S(1)}, u32[]{:S(2)}, u32[]{:S(2)}) collective-permute-start(f32[1,1024]{1,0:T(1,128)S(1)} %copy-done.7), channel_id=1, source_target_pairs={{0,4},{4,0},{8,12},{12,8},{16,20},{20,16},{24,28},{28,24},{1,5},{5... | collective-permute-start | bytes 12296 | tf_op jit(solution)/shard_map/ppermute | solution.py:387
  54.8 1.6 %collective-permute-start.7 = (bf16[128,1024]{1,0:T(8,128)(2,1)S(1)}, bf16[128,1024]{1,0:T(8,128)(2,1)S(1)}, u32[]{:S(2)}, u32[]{:S(2)}) collective-permute-start(bf16[128,1024]{1,0:T(8,128)(2,1)S(1)} %select_convert_fusion.3), channel_id=1, source_target_pairs={{0,4},{4,0},{8,12},{12,8},{16,20},{20,16},{24,28},{28,24},{1,5},{5... | collective-permute-start | bytes 786440 | tf_op jit(solution)/shard_map/ppermute | solution.py:387
  56.6 8.4 %collective-permute-start.8 = (bf16[128,1024]{1,0:T(8,128)(2,1)S(1)}, bf16[128,1024]{1,0:T(8,128)(2,1)S(1)}, u32[]{:S(2)}, u32[]{:S(2)}) collective-permute-start(bf16[128,1024]{1,0:T(8,128)(2,1)S(1)} %get-tuple-element.77), channel_id=1, source_target_pairs={{0,8},{4,12},{8,0},{12,4},{16,24},{20,28},{24,16},{28,20},{1,9},{5... | collective-permute-start | bytes 786440 | tf_op jit(solution)/shard_map/ppermute | solution.py:387
  65.1 8.5 %collective-permute-start.9 = (bf16[128,1024]{1,0:T(8,128)(2,1)S(1)}, bf16[128,1024]{1,0:T(8,128)(2,1)S(1)}, u32[]{:S(2)}, u32[]{:S(2)}) collective-permute-start(bf16[128,1024]{1,0:T(8,128)(2,1)S(1)} %fusion.5), channel_id=1, source_target_pairs={{0,16},{4,20},{8,24},{12,28},{16,0},{20,4},{24,8},{28,12},{1,17},{... | collective-permute-start | bytes 786440 | tf_op jit(solution)/shard_map/ppermute | solution.py:387
  66.7 3.4 %copy-start.2 = (bf16[1,1,4096,1024]{3,2,1,0:T(8,128)(2,1)S(1)}, bf16[1,1,4096,1024]{3,2,1,0:T(8,128)(2,1)}, u32[]{:S(2)}) copy-start(bf16[1,1,4096,1024]{3,2,1,0:T(8,128)(2,1)} %param.11) | copy-start | bytes 25165828
  74.1 1.6 %collective-permute-start.11 = (bf16[128,1024]{1,0:T(8,128)(2,1)S(1)}, bf16[128,1024]{1,0:T(8,128)(2,1)S(1)}, u32[]{:S(2)}, u32[]{:S(2)}) collective-permute-start(bf16[128,1024]{1,0:T(8,128)(2,1)S(1)} %select_convert_fusion.1), channel_id=1, source_target_pairs={{0,4},{4,0},{8,12},{12,8},{16,20},{20,16},{24,28},{28,24},{1,5},{5... | collective-permute-start | bytes 786440 | tf_op jit(solution)/shard_map/ppermute | solution.py:387
  74.2 2.3 %collective-permute-start.10 = (bf16[128,1024]{1,0:T(8,128)(2,1)S(1)}, bf16[128,1024]{1,0:T(8,128)(2,1)S(1)}, u32[]{:S(2)}, u32[]{:S(2)}) collective-permute-start(bf16[128,1024]{1,0:T(8,128)(2,1)S(1)} %get-tuple-element.73), channel_id=1, source_target_pairs={{0,4},{4,0},{8,12},{12,8},{16,20},{20,16},{24,28},{28,24},{1,5},{5... | collective-permute-start | bytes 786440 | tf_op jit(solution)/shard_map/ppermute | solution.py:387
  75.8 8.4 %collective-permute-start.12 = (bf16[128,1024]{1,0:T(8,128)(2,1)S(1)}, bf16[128,1024]{1,0:T(8,128)(2,1)S(1)}, u32[]{:S(2)}, u32[]{:S(2)}) collective-permute-start(bf16[128,1024]{1,0:T(8,128)(2,1)S(1)} %get-tuple-element.75), channel_id=1, source_target_pairs={{0,8},{4,12},{8,0},{12,4},{16,24},{20,28},{24,16},{28,20},{1,9},{5... | collective-permute-start | bytes 786440 | tf_op jit(solution)/shard_map/ppermute | solution.py:387
  84.4 7.6 %collective-permute-start.13 = (bf16[128,1024]{1,0:T(8,128)(2,1)S(1)}, bf16[128,1024]{1,0:T(8,128)(2,1)S(1)}, u32[]{:S(2)}, u32[]{:S(2)}) collective-permute-start(bf16[128,1024]{1,0:T(8,128)(2,1)S(1)} %fusion.8), channel_id=1, source_target_pairs={{0,16},{4,20},{8,24},{12,28},{16,0},{20,4},{24,8},{28,12},{1,17},{... | collective-permute-start | bytes 786440 | tf_op jit(solution)/shard_map/ppermute | solution.py:387
  85.1 14.7 %collective-permute-start.15 = (bf16[256,1024]{1,0:T(8,128)(2,1)S(1)}, bf16[256,1024]{1,0:T(8,128)(2,1)S(1)}, u32[]{:S(2)}, u32[]{:S(2)}) collective-permute-start(bf16[256,1024]{1,0:T(8,128)(2,1)S(1)} %fusion), channel_id=1, source_target_pairs={{0,1},{1,2},{2,3},{4,5},{5,6},{6,7},{8,9},{9,10},{10,11},{12,13},{... | collective-permute-start | bytes 1572872 | tf_op jit(solution)/shard_map/ppermute | solution.py:383
  92.2 7.6 %collective-permute-start.14 = (bf16[128,1024]{1,0:T(8,128)(2,1)S(1)}, bf16[128,1024]{1,0:T(8,128)(2,1)S(1)}, u32[]{:S(2)}, u32[]{:S(2)}) collective-permute-start(bf16[128,1024]{1,0:T(8,128)(2,1)S(1)} %select_convert_fusion), channel_id=1, source_target_pairs={{0,4},{4,0},{8,12},{12,8},{16,20},{20,16},{24,28},{28,24},{1,5},{5... | collective-permute-start | bytes 786440 | tf_op jit(solution)/shard_map/ppermute | solution.py:387
  92.3 20.0 %collective-permute-start.16 = (bf16[256,1024]{1,0:T(8,128)(2,1)S(1)}, bf16[256,1024]{1,0:T(8,128)(2,1)S(1)}, u32[]{:S(2)}, u32[]{:S(2)}) collective-permute-start(bf16[256,1024]{1,0:T(8,128)(2,1)S(1)} %fusion), channel_id=1, source_target_pairs={{1,0},{2,1},{3,2},{5,4},{6,5},{7,6},{9,8},{10,9},{11,10},{13,12},{... | collective-permute-start | bytes 1572872 | tf_op jit(solution)/shard_map/ppermute | solution.py:383
  100.3 13.8 %collective-permute-start.17 = (bf16[256,1024]{1,0:T(8,128)(2,1)S(1)}, bf16[256,1024]{1,0:T(8,128)(2,1)S(1)}, u32[]{:S(2)}, u32[]{:S(2)}) collective-permute-start(bf16[256,1024]{1,0:T(8,128)(2,1)S(1)} %fusion.1), channel_id=1, source_target_pairs={{0,1},{1,2},{2,3},{4,5},{5,6},{6,7},{8,9},{9,10},{10,11},{12,13},{... | collective-permute-start | bytes 1572872 | tf_op jit(solution)/shard_map/ppermute | solution.py:383
  114.1 16.1 %slice-start.4 = ((s8[8388608]{0:T(1024)(128)(4,1)}), s8[4194304]{0:T(1024)(128)(4,1)S(1)}, s32[]{:S(2)}) async-start(s8[8388608]{0:T(1024)(128)(4,1)} %bitcast.42), calls=%async_computation.4 | async-start | bytes 8388608
  115.1 14.4 %collective-permute-start.18 = (bf16[256,1152]{1,0:T(8,128)(2,1)S(1)}, bf16[256,1152]{1,0:T(8,128)(2,1)S(1)}, u32[]{:S(2)}, u32[]{:S(2)}) collective-permute-start(bf16[256,1152]{1,0:T(8,128)(2,1)S(1)} %message_part.3), channel_id=1, source_target_pairs={{0,1},{1,2},{2,3},{4,5},{5,6},{6,7},{8,9},{9,10},{10,11},{12,13},{... | collective-permute-start | bytes 1769480 | tf_op jit(solution)/shard_map/ppermute | solution.py:383
  117.7 12.5 %slice-start.5 = ((s8[8388608]{0:T(1024)(128)(4,1)}), s8[4194304]{0:T(1024)(128)(4,1)S(1)}, s32[]{:S(2)}) async-start(s8[8388608]{0:T(1024)(128)(4,1)} %bitcast.42), calls=%async_computation.5 | async-start | bytes 8388608
